TPU v7x, 256 devices: a whole 4x4x8 slice. The times are simulated.
256 devices in a mesh: segment: 2 (over core), expert: 32 (over y, z), tensor: 4 (over x).
Axes of the slice: x: 4, y: 4, z: 8, core: 2. Of those that a mesh axis runs over, the one named last changes fastest.
Arguments:
- activations: bfloat16 [2, 2048, 2560], P('segment', 'expert', 'tensor'), may hold values from -48 to 48
- expert_ids: int32 [2, 2048, 6], P(None, 'expert'), may hold values from 0 to 63, as said below
- route_weights: float32 [2, 2048, 6], P(None, 'expert'), may hold values from 0.05 to 1
- gain_dense: float32 [2560], replicated, may hold values from 0.25 to 1.75
- gain_expert: float32 [2560], replicated, may hold values from 0.25 to 1.75
- dense_gate: bfloat16 [2560, 6144], P('expert', 'tensor'), may hold values from -0.125 to 0.125
- dense_up: bfloat16 [2560, 6144], P('expert', 'tensor'), may hold values from -0.125 to 0.125
- dense_down: bfloat16 [2560, 6144], P('expert', 'tensor'), may hold values from -0.078125 to 0.078125
- expert_gate: bfloat16 [64, 2560, 1536], P('expert', None, 'tensor'), may hold values from -0.125 to 0.125
- expert_up: bfloat16 [64, 2560, 1536], P('expert', None, 'tensor'), may hold values from -0.125 to 0.125
- expert_down: bfloat16 [64, 1536, 2560], P('expert', 'tensor'), may hold values from -0.15625 to 0.15625
Outputs:
- sections: bfloat16 [2, 2, 2048, 2560], P('segment', None, 'expert', 'tensor')
Inputs may be any that keep to these rules, and one draw needn't show every extreme that they name: `expert_ids`: each token names 6 different experts. Split each micro-batch's tokens into blocks of 64 in order: no expert is named by more than 12 tokens of one block, and in every micro-batch one expert is named by exactly 12 tokens of every block.
All inputs are finite; a program needn't handle non-finite values.
Results may differ from a plain program's by a relative error of at most 0.009.
Values may be sent and summed in bfloat16 or wider, within the bound.
A program may use at most 128 MiB of HBM per device.

v0:
```python
import jax
import jax.numpy as jnp
from jax import lax
from jax.sharding import PartitionSpec as P

EPSILON = 1e-06


def shifted(block, axis, distance):
    devices = range(lax.axis_size(axis))
    route = [((i - distance) % len(devices), i) for i in devices]
    return lax.ppermute(block, axis, route)


def normalize(values, gain_row):
    inverse = lax.rsqrt(jnp.mean(values * values, axis=-1, keepdims=True) + EPSILON)
    return values * inverse * gain_row


def dense_prepare(micro_block, gain_dense):
    micro_count, tokens_here, quarter = micro_block.shape
    whole_rows = lax.all_gather(micro_block, "tensor", axis=2, tiled=True)
    full_width = whole_rows.shape[2]
    normed = normalize(whole_rows.astype(jnp.float32), gain_dense).astype(jnp.bfloat16)
    return normed.reshape(micro_count * tokens_here, full_width)


def dense_finish(micro_block, partial_value):
    micro_count, tokens_here, quarter = micro_block.shape
    summed = lax.psum_scatter(
        partial_value.reshape(micro_count, tokens_here, partial_value.shape[1]).astype(
            jnp.bfloat16
        ),
        "tensor",
        scatter_dimension=2,
        tiled=True,
    ).astype(jnp.float32)
    return (micro_block.astype(jnp.float32) + summed).astype(jnp.bfloat16)


def dense_folded(activations, gain_dense, dense_gate, dense_up, dense_down):
    normed = dense_prepare(activations, gain_dense)
    gate_sums = jnp.dot(
        normed,
        lax.all_gather(dense_gate, "expert", axis=0, tiled=True),
        preferred_element_type=jnp.float32,
    )
    upward = jnp.dot(
        normed,
        lax.all_gather(dense_up, "expert", axis=0, tiled=True),
        preferred_element_type=jnp.float32,
    )
    hidden = (jax.nn.silu(gate_sums) * upward).astype(jnp.bfloat16)
    partial_value = lax.dot_general(
        hidden,
        lax.all_gather(dense_down, "expert", axis=0, tiled=True),
        (((1,), (1,)), ((), ())),
        preferred_element_type=jnp.float32,
    )
    return dense_finish(activations, partial_value)


def route_slots(expert_ids_block, local_count, groups, capacity):
    tokens_here, picks = expert_ids_block.shape
    flat_ids = expert_ids_block.reshape(-1)
    experts_all = local_count * groups
    one_hot = (flat_ids[:, None] == jnp.arange(experts_all, dtype=jnp.int32)[None, :]).astype(
        jnp.int32
    )
    ranks = jnp.sum((jnp.cumsum(one_hot, axis=0) - 1) * one_hot, axis=1)
    slots = (flat_ids % local_count * groups + flat_ids // local_count) * capacity + ranks
    owners = jnp.arange(tokens_here * picks, dtype=jnp.int32) // picks
    sources = jnp.full((experts_all * capacity,), tokens_here, jnp.int32).at[slots].set(owners)
    return (slots, sources)


def place_rows(normed, sources, local_count, groups, capacity):
    padded = jnp.concatenate([normed, jnp.zeros((1, normed.shape[1]), normed.dtype)], axis=0)
    return padded[sources].reshape(local_count, groups, capacity, normed.shape[1])


def expert_block(
    middle, expert_ids_block, route_block, gain_expert, expert_gate, expert_up, expert_down
):
    tokens_here, quarter = middle.shape
    picks = expert_ids_block.shape[1]
    groups = lax.axis_size("expert")
    local_count, full_width, hidden_part = expert_gate.shape
    capacity = min(tokens_here, 2 * (tokens_here * picks // (local_count * groups)))
    slots, sources = route_slots(expert_ids_block, local_count, groups, capacity)
    middle_wide = middle.astype(jnp.float32)
    received_rows = groups * capacity
    tensor_index = lax.axis_index("tensor")
    square_sums = lax.psum(jnp.sum(middle_wide * middle_wide, axis=1), "tensor")
    inverse = lax.rsqrt(square_sums / full_width + EPSILON)
    gain_part = lax.dynamic_slice_in_dim(gain_expert, tensor_index * quarter, quarter, 0)
    normed = (middle_wide * inverse[:, None] * gain_part).astype(jnp.bfloat16)
    outgoing = place_rows(normed, sources, local_count, groups, capacity)
    arrived = lax.all_to_all(outgoing, "expert", split_axis=1, concat_axis=1, tiled=True)
    arrived = arrived.reshape(local_count, received_rows, quarter)
    slice_part = lax.all_gather(arrived, "tensor", axis=2, tiled=True)
    gate_sums = jnp.einsum(
        "lrc,lch->lrh", slice_part, expert_gate, preferred_element_type=jnp.float32
    )
    upward = jnp.einsum("lrc,lch->lrh", slice_part, expert_up, preferred_element_type=jnp.float32)
    hidden = (jax.nn.silu(gate_sums) * upward).astype(jnp.bfloat16)
    partial_value = jnp.einsum(
        "lrh,lhd->lrd", hidden, expert_down, preferred_element_type=jnp.float32
    )
    summed = lax.psum_scatter(
        partial_value.astype(jnp.bfloat16), "tensor", scatter_dimension=2, tiled=True
    )
    returned = lax.all_to_all(
        summed.reshape(local_count, groups, capacity, quarter),
        "expert",
        split_axis=1,
        concat_axis=1,
        tiled=True,
    )
    picked = returned.reshape(local_count * groups * capacity, quarter)[slots]
    picked = picked.reshape(tokens_here, picks, quarter).astype(jnp.float32)
    mixed = jnp.sum(route_block[:, :, None] * picked, axis=1)
    return (middle_wide + mixed).astype(jnp.bfloat16)


def body(
    activations,
    expert_ids,
    route_weights,
    gain_dense,
    gain_expert,
    dense_gate,
    dense_up,
    dense_down,
    expert_gate,
    expert_up,
    expert_down,
):
    segment_index = lax.axis_index("segment")
    own_middle = dense_folded(activations, gain_dense, dense_gate, dense_up, dense_down)
    other_middle = shifted(own_middle, "segment", 1)
    middles = jnp.where(
        segment_index == 0,
        jnp.concatenate([own_middle, other_middle], axis=0),
        jnp.concatenate([other_middle, own_middle], axis=0),
    )
    finals = jnp.stack(
        [
            expert_block(
                middles[position],
                expert_ids[position],
                route_weights[position],
                gain_expert,
                expert_gate,
                expert_up,
                expert_down,
            )
            for position in range(middles.shape[0])
        ]
    )
    sections = jnp.where(segment_index == 0, middles, finals)
    return sections[None]


def solution(mesh):
    placed = (
        P("segment", "expert", "tensor"),
        P(None, "expert", None),
        P(None, "expert", None),
        P(),
        P(),
        P("expert", "tensor"),
        P("expert", "tensor"),
        P("expert", "tensor"),
        P("expert", None, "tensor"),
        P("expert", None, "tensor"),
        P("expert", "tensor", None),
    )
    return jax.shard_map(
        body,
        mesh=mesh,
        in_specs=placed,
        out_specs=P("segment", None, "expert", "tensor"),
        check_vma=False,
    )
```

profile of v0, /device:TPU:1, one launch (start us, length us, event | category | flops | bytes accessed | tf_op | source)
XLA Modules:
  0.0 635.5 jit_solution(418148062136196478)
XLA Ops:
  11.0 11.5 %all_gather.18 = bf16[1,64,2560]{2,1,0:T(8,128)(2,1)S(1)} all-gather(bf16[1,64,640]{2,1,0:T(8,128)(2,1)} %param.11), channel_id=1, replica_groups=mesh['segment'=2,'expert'=32,'tensor'=4] {'tensor'}, dimensions={2}, use_global_device_ids=true | all-gather | bytes 409600 | tf_op jit(solution)/shard_map/all_gather | solution.py:22
  22.8 86.5 %all-gather.6.cloned.1.call-done = bf16[2560,1536]{1,0:T(8,128)(2,1)} async-done(((bf16[80,1536]{1,0:T(8,128)(2,1)}), bf16[2560,1536]{1,0:T(8,128)(2,1)}) %all-gather.6.cloned.1.call-update) | async-done | bytes 7864336 | tf_op jit(solution)/shard_map/all_gather | solution.py:45
  109.3 4.8 fusion.37
  114.0 90.8 %all-gather.10.cloned.1.call-done = bf16[2560,1536]{1,0:T(8,128)(2,1)} async-done(((bf16[80,1536]{1,0:T(8,128)(2,1)}), bf16[2560,1536]{1,0:T(8,128)(2,1)}) %all-gather.10.cloned.1.call-update) | async-done | bytes 7864336 | tf_op jit(solution)/shard_map/all_gather | solution.py:56
  204.8 95.6 %all-gather.8.cloned.1.call-done = bf16[2560,1536]{1,0:T(8,128)(2,1)} async-done(((bf16[80,1536]{1,0:T(8,128)(2,1)}), bf16[2560,1536]{1,0:T(8,128)(2,1)}) %all-gather.8.cloned.1.call-update) | async-done | bytes 7864336 | tf_op jit(solution)/shard_map/all_gather | solution.py:50
  300.5 9.4 %fusion = bf16[1,64,2560]{2,1,0:T(8,128)(2,1)S(1)} fusion(bf16[2560,1536]{1,0:T(8,128)(2,1)} %all-gather.10.cloned.1.call-done, bf16[2560,1536]{1,0:T(8,128)(2,1)} %all-gather.8.cloned.1.call-done, f32[64,1536]{1,0:T(8,128)S(1)} %fusion.37, bf16[1,64,2560]{2,1,0:T(8,128)(2,1)S(1)} %all_gather.18, f32[2560]{0:T(1024)S(1)} %copy-done.3, f32[64]{0:T(128)S(1)} %add_rsqrt_fusion.2), kind=kOutput, calls=%fused_computation.9 | convolution fusion | flops 1008041984 | bytes 16787712 | tf_op jit(solution)/shard_map/dot_general | solution.py:54
  309.8 1.0 copy.54
  310.8 0.9 copy.74
  313.6 2.9 scatter_custom_fusion.1
  316.5 15.6 %reduce-scatter.10.cloned.1.call-done = bf16[640,64]{1,0:T(8,128)(2,1)} async-done(((bf16[2560,64]{1,0:T(8,128)(2,1)}), bf16[640,64]{1,0:T(8,128)(2,1)}) %reduce-scatter.10.cloned.1.call-update) | async-done | bytes 81936
  332.1 1.1 reshape_bitcast_fusion
  333.4 2.4 collective-permute-start
  337.5 6.4 %all-reduce.2 = (f32[64]{0:T(128)S(1)}, f32[64]{0:T(128)S(1)}) all-reduce(f32[64]{0:T(128)S(1)} %get-tuple-element.5, f32[64]{0:T(128)S(1)} %get-tuple-element.6), channel_id=1, replica_groups=mesh['segment'=2,'expert'=32,'tensor'=4] {'tensor'}, use_global_device_ids=true, to_apply=%region_3.4 | all-reduce | flops 128 | bytes 1024 | tf_op jit(solution)/shard_map/psum | solution.py:94
  344.0 2.8 gather_fusion.2
  347.1 1.0 copy.50
  348.1 31.9 %all_to_all.20 = bf16[2,32,12,640]{3,0,2,1:T(2,128)(2,1)S(1)} all-to-all(bf16[2,32,12,640]{3,0,2,1:T(2,128)(2,1)S(1)} %copy.50), channel_id=1, replica_groups=mesh['segment'=2,'expert'=32,'tensor'=4] {'expert'}, dimensions={1} | all-to-all | bytes 1966080 | tf_op jit(solution)/shard_map/all_to_all | solution.py:99
  380.0 1.2 copy.51
  383.7 3.1 scatter_custom_fusion
  386.8 2.8 gather_fusion
  389.9 1.0 copy.40
  390.9 27.9 %all_to_all.21 = bf16[2,32,12,640]{3,0,2,1:T(2,128)(2,1)S(1)} all-to-all(bf16[2,32,12,640]{3,0,2,1:T(2,128)(2,1)S(1)} %copy.40), channel_id=1, replica_groups=mesh['segment'=2,'expert'=32,'tensor'=4] {'expert'}, dimensions={1} | all-to-all | bytes 1966080 | tf_op jit(solution)/shard_map/all_to_all | solution.py:99
  418.8 1.1 copy.41
  419.9 9.9 %all-gather.14.cloned.1.call-done = bf16[2,384,2560]{2,1,0:T(8,128)(2,1)} async-done(((bf16[2,384,640]{2,1,0:T(8,128)(2,1)}), bf16[2,384,2560]{2,1,0:T(8,128)(2,1)}) %all-gather.14.cloned.1.call-update) | async-done | bytes 3932176 | tf_op jit(solution)/shard_map/all_gather | solution.py:101
  429.8 5.5 fusion.60
  435.3 10.7 %convolution_convert_fusion = bf16[2,384,2560]{2,1,0:T(8,128)(2,1)} fusion(bf16[2,384,2560]{2,1,0:T(8,128)(2,1)} %param.21, bf16[2,384,2560]{2,1,0:T(8,128)(2,1)} %all-gather.14.cloned.1.call-done, bf16[2,2560,384]{2,1,0:T(8,128)(2,1)} %param.20, f32[2,384,384]{2,1,0:T(8,128)S(1)} %fusion.60), kind=kOutput, calls=%fused_computation.6 | convolution fusion | flops 3023634432 | bytes 16908288 | tf_op jit(solution)/shard_map/lrh,lhd->lrd/dot_general | solution.py:107
  446.0 10.7 %copy.58 = bf16[2,384,2560]{1,0,2:T(2,128)(2,1)} copy(bf16[2,384,2560]{2,1,0:T(8,128)(2,1)} %convolution_convert_fusion) | data formatting | bytes 7864320
  456.6 4.7 copy.70
  461.7 18.9 %all-gather.12.cloned.1.call-done = bf16[2,384,2560]{2,1,0:T(8,128)(2,1)} async-done(((bf16[2,384,640]{2,1,0:T(8,128)(2,1)}), bf16[2,384,2560]{2,1,0:T(8,128)(2,1)}) %all-gather.12.cloned.1.call-update) | async-done | bytes 3932176 | tf_op jit(solution)/shard_map/all_gather | solution.py:101
  480.5 5.5 fusion.59
  486.0 10.7 %convolution_convert_fusion.1 = bf16[2,384,2560]{2,1,0:T(8,128)(2,1)} fusion(bf16[2,384,2560]{2,1,0:T(8,128)(2,1)} %param.21, bf16[2,384,2560]{2,1,0:T(8,128)(2,1)} %all-gather.12.cloned.1.call-done, bf16[2,2560,384]{2,1,0:T(8,128)(2,1)} %param.20, f32[2,384,384]{2,1,0:T(8,128)S(1)} %fusion.59), kind=kOutput, calls=%fused_computation.7 | convolution fusion | flops 3023634432 | bytes 16908288 | tf_op jit(solution)/shard_map/lrh,lhd->lrd/dot_general | solution.py:107
  496.7 10.6 %copy.56 = bf16[2,384,2560]{1,0,2:T(2,128)(2,1)} copy(bf16[2,384,2560]{2,1,0:T(8,128)(2,1)} %convolution_convert_fusion.1) | data formatting | bytes 7864320
  507.3 4.7 copy.69
  512.0 18.8 %reduce-scatter.14.cloned.1.call-done = bf16[640,768]{1,0:T(8,128)(2,1)} async-done(((bf16[2560,768]{1,0:T(8,128)(2,1)}), bf16[640,768]{1,0:T(8,128)(2,1)}) %reduce-scatter.14.cloned.1.call-update) | async-done | bytes 983056
  530.7 2.3 reshape.494
  533.0 2.8 copy.52
  535.9 9.7 %all-to-all-start.3 = ((bf16[2,32,12,640]{3,0,2,1:T(2,128)(2,1)}), bf16[2,32,12,640]{3,0,2,1:T(2,128)(2,1)S(1)}, u32[]{:S(2)}, u32[]{:S(2)}) async-start(bf16[2,32,12,640]{3,0,2,1:T(2,128)(2,1)} %bitcast.15), calls=%async_computation.3 | async-start | bytes 1966080 | tf_op jit(solution)/shard_map/all_to_all | solution.py:113
  545.6 34.7 %reduce-scatter.12.cloned.1.call-done = bf16[640,768]{1,0:T(8,128)(2,1)} async-done(((bf16[2560,768]{1,0:T(8,128)(2,1)}), bf16[640,768]{1,0:T(8,128)(2,1)}) %reduce-scatter.12.cloned.1.call-update) | async-done | bytes 983056
  580.3 2.3 reshape.492
  582.6 2.9 copy.42
  585.5 9.6 %all-to-all-start.1 = ((bf16[2,32,12,640]{3,0,2,1:T(2,128)(2,1)}), bf16[2,32,12,640]{3,0,2,1:T(2,128)(2,1)S(1)}, u32[]{:S(2)}, u32[]{:S(2)}) async-start(bf16[2,32,12,640]{3,0,2,1:T(2,128)(2,1)} %bitcast.8), calls=%async_computation.1 | async-start | bytes 1966080 | tf_op jit(solution)/shard_map/all_to_all | solution.py:113
  597.5 2.8 gather_fusion.3
  600.3 1.2 reshape.438
  601.5 17.1 %all-to-all-done.1 = bf16[2,32,12,640]{3,0,2,1:T(2,128)(2,1)S(1)} async-done(((bf16[2,32,12,640]{3,0,2,1:T(2,128)(2,1)}), bf16[2,32,12,640]{3,0,2,1:T(2,128)(2,1)S(1)}, u32[]{:S(2)}, u32[]{:S(2)}) %all-to-all-start.1) | async-done | bytes 983072 | tf_op jit(solution)/shard_map/all_to_all | solution.py:113
  618.6 1.2 copy.43
  619.8 2.1 reshape.429
  622.0 2.5 gather_fusion.1
  624.5 1.2 reshape.436
  626.1 1.8 multiply_reduce_fusion.1
  (87 shorter events, 15.5 us)
Async XLA Ops:
  6.5 102.7 %all-gather.6.cloned.1.call-start = ((), (), s32[]{:S(2)}) async-start(), calls=%async_computation.7 | async-start | bytes 8110080 | tf_op jit(solution)/shard_map/all_gather | solution.py:45
  7.3 197.6 %all-gather.10.cloned.1.call-start = ((), (), s32[]{:S(2)}) async-start(), calls=%async_computation.9 | async-start | bytes 8110080 | tf_op jit(solution)/shard_map/all_gather | solution.py:56
  8.0 292.4 %all-gather.8.cloned.1.call-start = ((), (), s32[]{:S(2)}) async-start(), calls=%async_computation.8 | async-start | bytes 8110080 | tf_op jit(solution)/shard_map/all_gather | solution.py:50
  8.7 323.4 %reduce-scatter.10.cloned.1.call-start = ((), (), s32[]{:S(2)}) async-start(), calls=%async_computation.12 | async-start | bytes 819200
  22.7 277.7 %copy-start.3 = (f32[2560]{0:T(1024)S(1)}, f32[2560]{0:T(1024)}, u32[]{:S(2)}) copy-start(f32[2560]{0:T(1024)} %param.14) | copy-start | bytes 30724
  309.8 23.5 %copy-start.2 = (bf16[1,64,640]{2,1,0:T(8,128)(2,1)S(1)}, bf16[1,64,640]{2,1,0:T(8,128)(2,1)}, u32[]{:S(2)}) copy-start(bf16[1,64,640]{2,1,0:T(8,128)(2,1)} %param.11) | copy-start | bytes 245764
  311.7 118.1 %all-gather.14.cloned.1.call-start = ((), (), s32[]{:S(2)}) async-start(), calls=%async_computation.11 | async-start | bytes 4915200 | tf_op jit(solution)/shard_map/all_gather | solution.py:101
  313.0 0.6 copy-start.5
  333.4 3.3 collective-permute-start
  336.7 0.6 copy-start
  381.2 99.3 %all-gather.12.cloned.1.call-start = ((), (), s32[]{:S(2)}) async-start(), calls=%async_computation.10 | async-start | bytes 4915200 | tf_op jit(solution)/shard_map/all_gather | solution.py:101
  383.1 0.6 copy-start.7
  419.9 110.9 %reduce-scatter.14.cloned.1.call-start = ((), (), s32[]{:S(2)}) async-start(), calls=%async_computation.14 | async-start | bytes 4915200
  461.4 118.9 %reduce-scatter.12.cloned.1.call-start = ((), (), s32[]{:S(2)}) async-start(), calls=%async_computation.13 | async-start | bytes 4915200
  535.9 59.2 %copy-start.9 = (f32[2,64,6]{1,0,2:T(2,128)S(1)}, f32[2,64,6]{1,0,2:T(2,128)}, u32[]{:S(2)}) copy-start(f32[2,64,6]{1,0,2:T(2,128)} %param.13) | copy-start | bytes 9220
  535.9 60.0 %copy-start.6 = (s32[384]{0:T(512)S(1)}, s32[384]{0:T(512)}, u32[]{:S(2)}) copy-start(s32[384]{0:T(512)} %copy-done.5) | copy-start | bytes 4612
  535.9 60.6 %copy-start.8 = (s32[384]{0:T(512)S(1)}, s32[384]{0:T(512)}, u32[]{:S(2)}) copy-start(s32[384]{0:T(512)} %copy-done.7) | copy-start | bytes 4612
  535.9 49.6 %all-to-all-start.3 = ((bf16[2,32,12,640]{3,0,2,1:T(2,128)(2,1)}), bf16[2,32,12,640]{3,0,2,1:T(2,128)(2,1)S(1)}, u32[]{:S(2)}, u32[]{:S(2)}) async-start(bf16[2,32,12,640]{3,0,2,1:T(2,128)(2,1)} %bitcast.15), calls=%async_computation.3 | async-start | bytes 1966080 | tf_op jit(solution)/shard_map/all_to_all | solution.py:113
  585.5 33.1 %all-to-all-start.1 = ((bf16[2,32,12,640]{3,0,2,1:T(2,128)(2,1)}), bf16[2,32,12,640]{3,0,2,1:T(2,128)(2,1)S(1)}, u32[]{:S(2)}, u32[]{:S(2)}) async-start(bf16[2,32,12,640]{3,0,2,1:T(2,128)(2,1)} %bitcast.8), calls=%async_computation.1 | async-start | bytes 1966080 | tf_op jit(solution)/shard_map/all_to_all | solution.py:113
  622.0 4.1 copy-start.4
  622.0 6.0 copy-start.1
Sparse Core Ops, SparseCore 0:
  9.9 99.2 all-gather.5
  111.8 92.9 all-gather.9
  207.4 92.9 all-gather.7
  311.9 20.1 reduce-scatter.9
  381.3 48.4 all-gather.13
  431.5 48.9 all-gather.11
  483.1 47.6 reduce-scatter.13
  533.3 46.9 reduce-scatter.11
where the time goes:
time: 640 us; the launch traced here: 636 us
  waiting for transfers between devices  391 us (61%)
  blocking collectives  77.7 us (12%)
  local copies, waits for them, and re-layouts  77.5 us (12%)
  matrix products  46.4 us (7%)
  starting transfers between devices  22.2 us (3%)
  between operations  13.9 us (2%)
  other arithmetic  6.87 us (1%)
    all_gather x1, waiting for transfers between devices, dense_folded(): lax.all_gather(dense_up, 'expert', axis=0, tiled=True)  95.6 us
    all_gather x1, waiting for transfers between devices, dense_folded(): lax.all_gather(dense_down, 'expert', axis=0, tiled=True)  90.8 us
    all_gather x1, waiting for transfers between devices, dense_folded(): lax.all_gather(dense_gate, 'expert', axis=0, tiled=True)  86.5 us
    unnamed x11, waiting for transfers between devices  71.2 us
    all_to_all x2, blocking collectives, expert_block(): lax.all_to_all(outgoing, 'expert', split_axis=1, concat_axis=1, tiled=True)  59.8 us
    unnamed x30, local copies, waits for them, and re-layouts  40.2 us
    all_gather x2, waiting for transfers between devices, expert_block(): slice_part = lax.all_gather(arrived, 'tensor', axis=2, tiled=True)  28.8 us
    dot_general x2, matrix products, expert_block(): jnp.einsum('lrh,lhd->lrd', hidden, expert_down, preferred_element_type=jn...  21.3 us
  transfers between devices with their start and end apart: 11, of which 10 were waited for; matrix products, arithmetic and copies ran while one was open for 16% of the time, Pallas kernels for 0%

commit v1 on v0

v1 whole, which is shorter than its diff:
```python
import functools

import jax
import jax.numpy as jnp
from jax import lax
from jax.experimental import pallas as pl
from jax.experimental.pallas import tpu as pltpu
from jax.sharding import PartitionSpec as P

EPSILON = 1e-06
MESH = pl.DeviceIdType.MESH
CAP = 12
SPLIT = (4, 8)


def wait_bytes(ref, sem):
    pltpu.make_async_copy(ref, ref, sem).wait()


def places(split, tensors):
    ny, nz = split
    c, p, t = lax.axis_index("segment"), lax.axis_index("expert"), lax.axis_index("tensor")
    y, z = p // nz, p % nz

    def device(dc=0, dy=0, dz=0, dt=0):
        return (
            lax.rem(c + dc, 2),
            lax.rem(y + dy + ny, ny) * nz + lax.rem(z + dz + nz, nz),
            lax.rem(t + dt, tensors),
        )

    return c, p, t, y, z, device


def greet(offsets, device):
    barrier = pltpu.get_barrier_semaphore()
    for offset in offsets:
        pl.semaphore_signal(barrier, inc=1, device_id=device(*offset), device_id_type=MESH)
    pl.semaphore_wait(barrier, len(offsets))


def silu(v):
    return v / (1.0 + jnp.exp(-v))


def dense_kernel(
    split,
    tensors,
    x_ref,
    gain_ref,
    gate_ref,
    up_ref,
    down_ref,
    out_ref,
    xbuf,
    nbuf,
    wbuf,
    part,
    prec,
    tok_s,
    tok_r,
    w1_s,
    w1_r,
    ring_s,
    ring_r,
    sib_s,
    sib_r,
    out_s,
    out_r,
):
    ny, nz = split
    half = ny // 2
    c, p, t, y, z, device = places(split, tensors)
    tokens, quarter = x_ref.shape
    rows, width = wbuf.shape[2:]
    per_quarter = quarter // rows
    weights = (gate_ref, up_ref, down_ref)

    group = [(dy, dt) for dt in range(tensors) for dy in range(ny) if dy or dt]
    offsets = {(0, dy, 0, dt) for dy, dt in group} | {(1, 0, 0, 0)}
    offsets |= {(0, 0, 1, 0), (0, 0, nz - 1, 0)}
    greet(sorted(offsets), device)

    def first_hop():
        copies = []
        for dy in range(1, ny):
            there = lax.rem(y + dy, ny)
            for m in range(3):
                columns = pl.ds(pl.multiple_of(there * width, 128), width)
                copies.append(
                    pltpu.make_async_remote_copy(
                        src_ref=weights[m].at[:, columns],
                        dst_ref=wbuf.at[p, m],
                        send_sem=w1_s.at[dy - 1, m],
                        recv_sem=w1_r.at[lax.rem(y, half), m],
                        device_id=device(0, dy, 0, 0),
                        device_id_type=MESH,
                    )
                )
        return copies

    sends_weights = y // half == c

    @pl.when(sends_weights)
    def _():
        for copy in first_hop():
            copy.start()
        for m in range(3):
            columns = pl.ds(pl.multiple_of(y * width, 128), width)
            pltpu.make_async_copy(
                weights[m].at[:, columns], wbuf.at[p, m], w1_r.at[lax.rem(y, half), m]
            ).start()

    token_copies = []
    for i, (dy, dt) in enumerate(group):
        token_copies.append(
            pltpu.make_async_remote_copy(
                src_ref=x_ref,
                dst_ref=xbuf.at[t, y],
                send_sem=tok_s.at[i],
                recv_sem=tok_r.at[i],
                device_id=device(0, dy, 0, dt),
                device_id_type=MESH,
            )
        )
        token_copies[-1].start()
    xbuf[t, y] = x_ref[...]

    right, left = 0, 1
    hops = {}
    for a in range(half):
        far, near = nz // 2, (nz - 1) // 2
        hops[right, a], hops[left, a] = (far, near) if a % 2 == 0 else (near, far)
    started = []

    def piece(a, dz):
        return (half * c + a) * nz + lax.rem(z + dz + nz, nz)

    def forward(direction, a, step):
        sign = 1 if direction == right else -1
        at = piece(a, -sign * (step - 1))
        copy = pltpu.make_async_remote_copy(
            src_ref=wbuf.at[at],
            dst_ref=wbuf.at[at],
            send_sem=ring_s.at[direction, a, step - 1],
            recv_sem=ring_r.at[direction, a, step - 1],
            device_id=device(0, 0, sign if sign > 0 else nz - 1, 0),
            device_id_type=MESH,
        )
        copy.start()
        started.append(copy)

    def share(a, dz):
        at = piece(a, dz)
        copy = pltpu.make_async_remote_copy(
            src_ref=wbuf.at[at],
            dst_ref=wbuf.at[at],
            send_sem=sib_s.at[a, dz % nz],
            recv_sem=sib_r.at[a, dz % nz],
            device_id=device(1, 0, 0, 0),
            device_id_type=MESH,
        )
        copy.start()
        started.append(copy)

    for a in range(half):
        for m in range(3):
            wait_bytes(wbuf.at[piece(a, 0), m], w1_r.at[a, m])
        for direction in (right, left):
            if hops[direction, a] >= 1:
                forward(direction, a, 1)
        share(a, 0)

    for i in range(len(group)):
        wait_bytes(xbuf.at[0, 0], tok_r.at[i])

    def norm_block(j, carry):
        squares = jnp.zeros((tokens, 1), jnp.float32)
        for q in range(tensors):
            values = xbuf[q, j].astype(jnp.float32)
            squares += jnp.sum(values * values, axis=1, keepdims=True)
        inverse = lax.rsqrt(squares / (quarter * tensors) + EPSILON)
        for q in range(tensors):
            values = xbuf[q, j].astype(jnp.float32)
            nbuf[q, j] = (values * inverse * gain_ref[q]).astype(jnp.bfloat16)
        return carry

    for step in range(1, nz // 2 + 1):
        for a in range(half):
            for direction in (right, left):
                if step > hops[direction, a]:
                    continue
                sign = 1 if direction == right else -1
                wait_bytes(wbuf.at[piece(a, -sign * step)], ring_r.at[direction, a, step - 1])
                if step + 1 <= hops[direction, a]:
                    forward(direction, a, step + 1)
                share(a, -sign * step)
        if step == 1:
            lax.fori_loop(0, ny, norm_block, 0)
    for a in range(half):
        for dz in range(nz):
            at = (half * (1 - c) + a) * nz + lax.rem(z + dz, nz)
            wait_bytes(wbuf.at[at], sib_r.at[a, dz])

    gate_sums = jnp.zeros((ny * tokens, width), jnp.float32)
    upward = jnp.zeros((ny * tokens, width), jnp.float32)
    for q in range(tensors):
        normed = nbuf[q].reshape(ny * tokens, quarter)
        held = pl.ds(q * per_quarter, per_quarter)
        gate_sums += jnp.dot(
            normed, wbuf[held, 0].reshape(quarter, width), preferred_element_type=jnp.float32
        )
        upward += jnp.dot(
            normed, wbuf[held, 1].reshape(quarter, width), preferred_element_type=jnp.float32
        )
    hidden = (silu(gate_sums) * upward).astype(jnp.bfloat16)

    order = [dt for dt in range(tensors) if dt] + [0]
    for dt in order:
        there = lax.rem(t + dt, tensors)
        down = wbuf[pl.ds(there * per_quarter, per_quarter), 2].reshape(quarter, width)
        result = lax.dot_general(
            hidden, down, (((1,), (1,)), ((), ())), preferred_element_type=jnp.float32
        )
        part[dt] = result.astype(jnp.bfloat16).reshape(ny, tokens, quarter)
        for i, (dy, other) in enumerate(group):
            if other != dt:
                continue
            copy = pltpu.make_async_remote_copy(
                src_ref=part.at[dt, lax.rem(y + dy, ny)],
                dst_ref=prec.at[i],
                send_sem=out_s.at[i],
                recv_sem=out_r.at[i],
                device_id=device(0, dy, 0, dt),
                device_id_type=MESH,
            )
            copy.start()
            started.append(copy)
    total = x_ref[...].astype(jnp.float32)
    summed = part[0, y].astype(jnp.float32)
    for i in range(len(group)):
        wait_bytes(prec.at[i], out_r.at[i])
        summed += prec[i].astype(jnp.float32)
    out_ref[...] = (total + summed).astype(jnp.bfloat16)

    for copy in token_copies + started:
        copy.wait_send()

    @pl.when(sends_weights)
    def _():
        for copy in first_hop():
            copy.wait_send()


def dense_section(x, gain, gate, up, down, split, tensors):
    ny, nz = split
    half = ny // 2
    tokens, quarter = x.shape
    rows, hidden = gate.shape
    width = hidden // ny
    group = ny * tensors - 1
    dma = pltpu.SemaphoreType.DMA
    vmem = pl.BlockSpec(memory_space=pltpu.VMEM)
    return pl.pallas_call(
        functools.partial(dense_kernel, split, tensors),
        out_shape=jax.ShapeDtypeStruct((tokens, quarter), jnp.bfloat16),
        in_specs=[vmem] * 5,
        out_specs=vmem,
        scratch_shapes=[
            pltpu.VMEM((tensors, ny, tokens, quarter), jnp.bfloat16),
            pltpu.VMEM((tensors, ny, tokens, quarter), jnp.bfloat16),
            pltpu.VMEM((ny * nz, 3, rows, width), jnp.bfloat16),
            pltpu.VMEM((tensors, ny, tokens, quarter), jnp.bfloat16),
            pltpu.VMEM((group, tokens, quarter), jnp.bfloat16),
            dma((group,)),
            dma((group,)),
            dma((ny - 1, 3)),
            dma((half, 3)),
            dma((2, half, nz // 2)),
            dma((2, half, nz // 2)),
            dma((half, nz)),
            dma((half, nz)),
            dma((group,)),
            dma((group,)),
        ],
        compiler_params=pltpu.CompilerParams(
            collective_id=0, has_side_effects=True, vmem_limit_bytes=48 * 2**20
        ),
        name="dense_section",
    )(x, gain, gate, up, down)


def expert_kernel(
    split,
    tensors,
    middle_ref,
    ids_ref,
    route_ref,
    gain_ref,
    gate_hbm,
    up_hbm,
    down_hbm,
    out_ref,
    gate,
    up,
    down,
    mids,
    sums,
    outgoing,
    arrived,
    pieces,
    pieces_in,
    summed,
    returned,
    mixes,
    w_sem,
    mid_s,
    mid_r,
    sum_s,
    sum_r,
    go_s,
    go_r,
    x_s,
    x_r,
    piece_s,
    piece_r,
    back_s,
    back_r,
    mix_s,
    mix_r,
):
    ny, nz = split
    chips = ny * nz
    c, p, t, y, z, device = places(split, tensors)
    tokens, quarter = middle_ref.shape
    slots = 2 * CAP
    all_slots = chips * slots
    hidden_width = gate.shape[1]

    loads = [
        pltpu.make_async_copy(far.at[c], near, w_sem.at[i])
        for i, (far, near) in enumerate(((gate_hbm, gate), (up_hbm, up), (down_hbm, down)))
    ]
    for load in loads:
        load.start()

    offsets = {(0, dy, dz, 0) for dy in range(ny) for dz in range(nz) if dy or dz}
    offsets |= {(dc, 0, 0, dt) for dc in range(2) for dt in range(tensors) if dc or dt}
    greet(sorted(offsets), device)

    own = middle_ref[...]
    mids[c] = own
    wide = own.astype(jnp.float32)
    sums[t, c] = jnp.broadcast_to(jnp.sum(wide * wide, axis=1, keepdims=True), (tokens, 128))
    started = []
    mid_copy = pltpu.make_async_remote_copy(
        src_ref=mids.at[c],
        dst_ref=mids.at[c],
        send_sem=mid_s,
        recv_sem=mid_r,
        device_id=device(1, 0, 0, 0),
        device_id_type=MESH,
    )
    mid_copy.start()
    started.append(mid_copy)
    others = [(dc, dt) for dc in range(2) for dt in range(tensors) if dc or dt]
    for i, (dc, dt) in enumerate(others):
        copy = pltpu.make_async_remote_copy(
            src_ref=sums.at[t, c],
            dst_ref=sums.at[t, c],
            send_sem=sum_s.at[i],
            recv_sem=sum_r.at[i],
            device_id=device(dc, 0, 0, dt),
            device_id_type=MESH,
        )
        copy.start()
        started.append(copy)

    def expert_at(k):
        there = lax.rem(y + k // nz, ny) * nz + lax.rem(z + k % nz, nz)
        return 2 * there + c

    experts = expert_at(lax.broadcasted_iota(jnp.int32, (2 * tokens, chips), 1))
    named = jnp.zeros((2 * tokens, chips), jnp.float32)
    share = jnp.zeros((2 * tokens, chips), jnp.float32)
    for j in range(ids_ref.shape[1]):
        same = ids_ref[:, j : j + 1] == experts
        named += jnp.where(same, 1.0, 0.0)
        share += jnp.where(same, route_ref[:, j : j + 1], 0.0)
    one = lax.broadcasted_iota(jnp.int32, (2 * tokens, 2 * tokens), 0)
    two = lax.broadcasted_iota(jnp.int32, (2 * tokens, 2 * tokens), 1)
    before = jnp.where((two < one) & (two // tokens == one // tokens), 1.0, 0.0)
    ranks = jnp.dot(
        before.astype(jnp.bfloat16), named.astype(jnp.bfloat16), preferred_element_type=jnp.float32
    )
    ranks = jnp.where(named > 0.5, ranks, -1.0).astype(jnp.bfloat16)
    share_high = share.astype(jnp.bfloat16)
    share_low = (share - share_high.astype(jnp.float32)).astype(jnp.bfloat16)

    def chooses(shape, slot_axis):
        slot = lax.broadcasted_iota(jnp.int32, shape, slot_axis)
        other = lax.broadcasted_iota(jnp.int32, shape, 1 - slot_axis)
        return slot, other

    slot, chip = chooses((chips, all_slots), 1)
    spread = jnp.where(slot // slots == chip, 1.0, 0.0).astype(jnp.bfloat16)
    slot, chip = chooses((all_slots, chips), 0)
    spread_t = jnp.where(slot // slots == chip, 1.0, 0.0).astype(jnp.bfloat16)

    def is_chosen(found, slot, row):
        rank = (slot % CAP).astype(jnp.float32)
        return (found == rank) & ((slot // CAP) % 2 == row // tokens)

    slot, row = chooses((all_slots, 2 * tokens), 0)
    found = lax.dot_general(
        spread_t, ranks, (((1,), (1,)), ((), ())), preferred_element_type=jnp.float32
    )
    place = jnp.where(is_chosen(found, slot, row), 1.0, 0.0).astype(jnp.bfloat16)

    wait_bytes(mids.at[0], mid_r)
    for i in range(len(others)):
        wait_bytes(sums.at[0, 0], sum_r.at[i])
    normed = []
    for m in range(2):
        squares = sums[0, m]
        for q in range(1, tensors):
            squares += sums[q, m]
        inverse = lax.rsqrt(squares[:, :1] / (quarter * tensors) + EPSILON)
        normed.append(
            (mids[m].astype(jnp.float32) * inverse * gain_ref[t]).astype(jnp.bfloat16)
        )
    normed = jnp.concatenate(normed, axis=0)
    for dy in range(ny):
        rows = place[dy * nz * slots : (dy + 1) * nz * slots]
        block = jnp.dot(rows, normed, preferred_element_type=jnp.float32)
        block = block.reshape(nz, slots, quarter).astype(jnp.bfloat16)
        outgoing[pl.ds(dy * nz, nz)] = block
        if dy == 0:
            arrived[t, 0] = block[0]

        def send(dz, carry, dy=dy):
            k = dy * nz + dz
            pltpu.make_async_remote_copy(
                src_ref=outgoing.at[k],
                dst_ref=arrived.at[t, k],
                send_sem=go_s.at[k],
                recv_sem=go_r.at[k],
                device_id=device(0, dy, dz, 0),
                device_id_type=MESH,
            ).start()
            return carry

        lax.fori_loop(1 if dy == 0 else 0, nz, send, 0)

    for load in loads:
        load.wait()

    def share_chunk(chunk):
        def arrive(dz, carry):
            k = chunk * nz + dz

            @pl.when(k > 0)
            def _():
                wait_bytes(arrived.at[t, k], go_r.at[k])

            return carry

        lax.fori_loop(0, nz, arrive, 0)
        for dt in range(1, tensors):
            held = arrived.at[t, pl.ds(chunk * nz, nz)]
            pltpu.make_async_remote_copy(
                src_ref=held,
                dst_ref=held,
                send_sem=x_s.at[dt - 1, chunk],
                recv_sem=x_r.at[dt - 1, chunk],
                device_id=device(0, 0, 0, dt),
                device_id_type=MESH,
            ).start()

    def compute_chunk(chunk):
        here = pl.ds(chunk * nz, nz)
        for dt in range(1, tensors):
            wait_bytes(arrived.at[0, here], x_r.at[dt - 1, chunk])
        gate_sums = jnp.zeros((nz * slots, hidden_width), jnp.float32)
        upward = jnp.zeros((nz * slots, hidden_width), jnp.float32)
        for q in range(tensors):
            values = arrived[q, here].reshape(nz * slots, quarter)
            some = slice(q * quarter, (q + 1) * quarter)
            gate_sums += jnp.dot(values, gate[some], preferred_element_type=jnp.float32)
            upward += jnp.dot(values, up[some], preferred_element_type=jnp.float32)
        hidden = (silu(gate_sums) * upward).astype(jnp.bfloat16)
        for dt in [*range(1, tensors), 0]:
            there = lax.rem(t + dt, tensors)
            columns = pl.ds(pl.multiple_of(there * quarter, 128), quarter)
            result = jnp.dot(hidden, down[:, columns], preferred_element_type=jnp.float32)
            pieces[dt, here] = result.reshape(nz, slots, quarter).astype(jnp.bfloat16)
            if dt:
                pltpu.make_async_remote_copy(
                    src_ref=pieces.at[dt, here],
                    dst_ref=pieces_in.at[dt - 1, here],
                    send_sem=piece_s.at[dt - 1, chunk],
                    recv_sem=piece_r.at[dt - 1, chunk],
                    device_id=device(0, 0, 0, dt),
                    device_id_type=MESH,
                ).start()

    def return_chunk(chunk):
        here = pl.ds(chunk * nz, nz)
        total = pieces[0, here].astype(jnp.float32)
        for dt in range(1, tensors):
            wait_bytes(pieces_in.at[dt - 1, here], piece_r.at[dt - 1, chunk])
            total += pieces_in[dt - 1, here].astype(jnp.float32)
        summed[here] = total.astype(jnp.bfloat16)

        def give(dz, carry):
            k = chunk * nz + dz

            @pl.when(k > 0)
            def _():
                pltpu.make_async_remote_copy(
                    src_ref=summed.at[k],
                    dst_ref=returned.at[k],
                    send_sem=back_s.at[k],
                    recv_sem=back_r.at[k],
                    device_id=device(0, ny - chunk, nz - dz, 0),
                    device_id_type=MESH,
                ).start()

            return carry

        lax.fori_loop(0, nz, give, 0)

    def stage(i, carry):
        @pl.when(i < ny)
        def _():
            share_chunk(i)

        @pl.when((i >= 1) & (i <= ny))
        def _():
            compute_chunk(i - 1)

        @pl.when(i >= 2)
        def _():
            return_chunk(i - 2)

        return carry

    lax.fori_loop(0, ny + 2, stage, 0)
    returned[0] = summed[0]

    slot, row = chooses((2 * tokens, all_slots), 1)
    row, slot = slot, row
    slot = lax.broadcasted_iota(jnp.int32, (2 * tokens, all_slots), 1)
    row = lax.broadcasted_iota(jnp.int32, (2 * tokens, all_slots), 0)
    found = jnp.dot(ranks, spread, preferred_element_type=jnp.float32)
    chosen = is_chosen(found, slot, row)
    mixers = []
    for part in (share_high, share_low):
        values = jnp.dot(part, spread, preferred_element_type=jnp.float32)
        mixers.append(jnp.where(chosen, values, 0.0).astype(jnp.bfloat16))

    def arrive_back(k, carry):
        wait_bytes(returned.at[k], back_r.at[k])
        return carry

    lax.fori_loop(1, chips, arrive_back, 0)
    back = returned[...].reshape(all_slots, quarter)
    mixed = jnp.dot(mixers[0], back, preferred_element_type=jnp.float32)
    mixed += jnp.dot(mixers[1], back, preferred_element_type=jnp.float32)
    mixes[0] = mixed
    mix_copy = pltpu.make_async_remote_copy(
        src_ref=mixes.at[0],
        dst_ref=mixes.at[1],
        send_sem=mix_s,
        recv_sem=mix_r,
        device_id=device(1, 0, 0, 0),
        device_id_type=MESH,
    )
    mix_copy.start()
    mix_copy.wait_recv()
    both = mixes[0] + mixes[1]
    for m in range(2):
        first = mids[m]
        final = first.astype(jnp.float32) + both[m * tokens : (m + 1) * tokens]
        out_ref[m] = jnp.where(c == 0, first, final.astype(jnp.bfloat16))

    mix_copy.wait_send()
    for copy in started:
        copy.wait_send()

    def sent(k, carry):
        wait_bytes(outgoing.at[k], go_s.at[k])
        wait_bytes(summed.at[k], back_s.at[k])
        return carry

    lax.fori_loop(1, chips, sent, 0)

    def sent_chunk(chunk, carry):
        here = pl.ds(chunk * nz, nz)
        for dt in range(1, tensors):
            wait_bytes(arrived.at[t, here], x_s.at[dt - 1, chunk])
            wait_bytes(pieces.at[dt, here], piece_s.at[dt - 1, chunk])
        return carry

    lax.fori_loop(0, ny, sent_chunk, 0)


def expert_section(middle, ids, route, gain, gate, up, down, split, tensors):
    ny, nz = split
    chips = ny * nz
    tokens, quarter = middle.shape
    slots = 2 * CAP
    hidden = gate.shape[2]
    full = quarter * tensors
    dma = pltpu.SemaphoreType.DMA
    vmem = pl.BlockSpec(memory_space=pltpu.VMEM)
    hbm = pl.BlockSpec(memory_space=pl.ANY)
    rows = (chips, slots, quarter)
    return pl.pallas_call(
        functools.partial(expert_kernel, split, tensors),
        out_shape=jax.ShapeDtypeStruct((2, tokens, quarter), jnp.bfloat16),
        in_specs=[vmem] * 4 + [hbm] * 3,
        out_specs=vmem,
        scratch_shapes=[
            pltpu.VMEM((full, hidden), jnp.bfloat16),
            pltpu.VMEM((full, hidden), jnp.bfloat16),
            pltpu.VMEM((hidden, full), jnp.bfloat16),
            pltpu.VMEM((2, tokens, quarter), jnp.bfloat16),
            pltpu.VMEM((tensors, 2, tokens, 128), jnp.float32),
            pltpu.VMEM(rows, jnp.bfloat16),
            pltpu.VMEM((tensors, *rows), jnp.bfloat16),
            pltpu.VMEM((tensors, *rows), jnp.bfloat16),
            pltpu.VMEM((tensors - 1, *rows), jnp.bfloat16),
            pltpu.VMEM(rows, jnp.bfloat16),
            pltpu.VMEM(rows, jnp.bfloat16),
            pltpu.VMEM((2, 2 * tokens, quarter), jnp.float32),
            dma((3,)),
            dma(()),
            dma(()),
            dma((2 * tensors - 1,)),
            dma((2 * tensors - 1,)),
            dma((chips,)),
            dma((chips,)),
            dma((tensors - 1, ny)),
            dma((tensors - 1, ny)),
            dma((tensors - 1, ny)),
            dma((tensors - 1, ny)),
            dma((chips,)),
            dma((chips,)),
            dma(()),
            dma(()),
        ],
        compiler_params=pltpu.CompilerParams(
            collective_id=1, has_side_effects=True, vmem_limit_bytes=56 * 2**20
        ),
        name="expert_section",
    )(middle, ids, route, gain, gate, up, down)


def body(
    split,
    tensors,
    activations,
    expert_ids,
    route_weights,
    gain_dense,
    gain_expert,
    dense_gate,
    dense_up,
    dense_down,
    expert_gate,
    expert_up,
    expert_down,
):
    tokens, quarter = activations.shape[1:]
    picks = expert_ids.shape[2]
    middle = dense_section(
        activations[0],
        gain_dense.reshape(tensors, 1, quarter),
        dense_gate,
        dense_up,
        dense_down,
        split,
        tensors,
    )
    sections = expert_section(
        middle,
        expert_ids.reshape(2 * tokens, picks),
        route_weights.reshape(2 * tokens, picks),
        gain_expert.reshape(tensors, 1, quarter),
        expert_gate,
        expert_up,
        expert_down,
        split,
        tensors,
    )
    return sections[None]


def solution(mesh, split=SPLIT):
    placed = (
        P("segment", "expert", "tensor"),
        P(None, "expert", None),
        P(None, "expert", None),
        P(),
        P(),
        P("expert", "tensor"),
        P("expert", "tensor"),
        P("expert", "tensor"),
        P("expert", None, "tensor"),
        P("expert", None, "tensor"),
        P("expert", "tensor", None),
    )
    return jax.shard_map(
        functools.partial(body, split, mesh.shape["tensor"]),
        mesh=mesh,
        in_specs=placed,
        out_specs=P("segment", None, "expert", "tensor"),
        check_vma=False,
    )
```

time: 640 us -> 213 us (0.33)
  waiting for transfers between devices: 391 us -> 0 us
  Pallas kernels: 0 us -> 201 us
  blocking collectives: 77.7 us -> 0 us
  local copies, waits for them, and re-layouts: 77.5 us -> 10.8 us
  matrix products: 46.4 us -> 0 us
  starting transfers between devices: 22.2 us -> 0 us
  between operations: 13.9 us -> 0.03 us
  other arithmetic: 6.87 us -> 0 us
    all_gather x5 -> x0, waiting for transfers between devices: 302 us -> none  [the longest x1 95.6 us: dense_folded(): lax.all_gather(dense_up, 'expert', axis=0, tiled=True)]
    pallas_call x0 -> x2, Pallas kernels: none -> 201 us  [the longest x1 121 us: expert_section(): pl.pallas_call(functools.partial(expert_kernel, split, tensors), out_shap...]
    unnamed x11 -> x0, waiting for transfers between devices: 71.2 us -> none
    all_to_all x2 -> x0, blocking collectives: 59.8 us -> none  [expert_block(): lax.all_to_all(outgoing, 'expert', split_axis=1, concat_axis=1, tiled=True)]
    dot_general x6 -> x0, matrix products: 46.4 us -> none  [the longest x2 21.3 us: expert_block(): jnp.einsum('lrh,lhd->lrd', hidden, expert_down, preferred_element_type=jn...]
    unnamed x30 -> x13, local copies, waits for them, and re-layouts: 40.2 us -> 8.79 us
    all_to_all x2 -> x0, starting transfers between devices: 19.3 us -> none  [expert_block(): lax.all_to_all(summed.reshape(local_count, groups, capacity, quarter), 'e...]
    all_to_all x2 -> x0, waiting for transfers between devices: 17.1 us -> none  [expert_block(): lax.all_to_all(summed.reshape(local_count, groups, capacity, quarter), 'e...]
  transfers between devices with their start and end apart: 11 -> 0, of which waited for: 10 -> 0; matrix products, arithmetic and copies ran while one was open for 16% -> 0% of each run, Pallas kernels for 0% -> 0%
where the time goes in v1:
time: 213 us; the launch traced here: 212 us
  Pallas kernels  201 us (94%)
  local copies, waits for them, and re-layouts  10.8 us (5%)
    pallas_call x1, Pallas kernels, expert_section(): pl.pallas_call(functools.partial(expert_kernel, split, tensors), out_shap...  121 us
    pallas_call x1, Pallas kernels, dense_section(): pl.pallas_call(functools.partial(dense_kernel, split, tensors), out_shape...  80.3 us
    unnamed x13, local copies, waits for them, and re-layouts  8.79 us

profile of v1, /device:TPU:1, one launch (start us, length us, event | category | flops | bytes accessed | tf_op | source)
XLA Modules:
  0.0 212.2 jit_solution(11693180566436514966)
XLA Ops:
  0.0 0.7 reshape.12.gain_ref
  0.7 1.3 reshape.15.gain_ref
  2.0 1.4 copy.12
  3.5 1.4 copy.13
  4.9 0.0 copy-start.1
  4.9 0.9 copy-done.1
  5.8 0.0 copy-start.2
  5.8 0.9 copy-done.2
  6.8 0.0 copy-start.3
  6.8 0.9 copy-done.3
  7.7 0.0 copy-start.4
  7.7 0.9 copy-done.4
  8.6 80.3 %dense_section.1.middle_ref = bf16[64,640]{1,0:T(8,128)(2,1)S(1)} custom-call(bf16[64,640]{1,0:T(8,128)(2,1)S(1)} %bitcast.4, f32[4,1,640]{2,1,0:T(1,128)S(1)} %reshape.12.gain_ref, bf16[80,1536]{1,0:T(8,128)(2,1)S(1)} %copy-done.1, bf16[80,1536]{1,0:T(8,128)(2,1)S(1)} %copy-done.2, bf16[80,1536]{1,0:T(8,128)(2,1)S(1)} %copy-done.3), custom_call_target="tpu_custom_call" | custom-call | tf_op jit(solution)/shard_map/dense_section/pallas_call | solution.py:264
  88.9 0.0 copy-start
  88.9 0.6 copy-done
  89.5 121.1 %expert_section.1 = bf16[2,64,640]{2,1,0:T(8,128)(2,1)} custom-call(bf16[64,640]{1,0:T(8,128)(2,1)} %copy-done, s32[128,6]{1,0:T(8,128)} %bitcast.6, f32[128,6]{1,0:T(8,128)} %bitcast.7, f32[4,1,640]{2,1,0:T(1,128)} %reshape.15.gain_ref, bf16[2,2560,384]{2,1,0:T(8,128)(2,1)} %gate_hbm.1, bf16[2,2560,384]{2,1,0:T(8,128)(2,1)} %up_hbm.1, ...), custom_call_target="tpu_custom_call" | custom-call | tf_op jit(solution)/shard_map/expert_section/pallas_call | solution.py:619
  210.6 1.6 copy.15
Async XLA Ops:
  4.9 0.9 copy-start.1
  5.8 0.9 copy-start.2
  6.8 0.9 copy-start.3
  7.7 0.9 copy-start.4
  88.9 0.6 copy-start

commit v2 on v0

v2 whole, which is shorter than its diff:
```python
import functools

import jax
import jax.numpy as jnp
from jax import lax
from jax.experimental import pallas as pl
from jax.experimental.pallas import tpu as pltpu
from jax.sharding import PartitionSpec as P

EPSILON = 1e-06
MESH = pl.DeviceIdType.MESH
CAP = 12
SPLIT = (4, 8)


def wait_bytes(ref, sem):
    pltpu.make_async_copy(ref, ref, sem).wait()


def places(split, tensors):
    ny, nz = split
    c, p, t = lax.axis_index("segment"), lax.axis_index("expert"), lax.axis_index("tensor")
    y, z = p // nz, p % nz

    def device(dc=0, dy=0, dz=0, dt=0):
        return (
            lax.rem(c + dc, 2),
            lax.rem(y + dy + ny, ny) * nz + lax.rem(z + dz + nz, nz),
            lax.rem(t + dt, tensors),
        )

    return c, p, t, y, z, device


def greet(offsets, device):
    barrier = pltpu.get_barrier_semaphore()
    for offset in offsets:
        pl.semaphore_signal(barrier, inc=1, device_id=device(*offset), device_id_type=MESH)
    pl.semaphore_wait(barrier, len(offsets))


def silu(v):
    return v / (1.0 + jnp.exp(-v))


def kernel(
    split,
    tensors,
    x_hbm,
    ids_ref,
    route_ref,
    gain_dense_ref,
    gain_expert_ref,
    dense_gate_hbm,
    dense_up_hbm,
    dense_down_hbm,
    gate_hbm,
    up_hbm,
    down_hbm,
    out_ref,
    x_ref,
    dense_held,
    xbuf,
    wbuf,
    hidden_ref,
    part,
    prec,
    gate,
    up,
    down,
    place,
    mixers,
    mids,
    sums,
    outgoing,
    arrived,
    pieces,
    through,
    beside,
    summed,
    returned,
    mixes,
    load_sem,
    tok_s,
    tok_r,
    w1_s,
    w1_r,
    ring_s,
    ring_r,
    sib_s,
    sib_r,
    out_s,
    out_r,
    mid_s,
    mid_r,
    sum_s,
    sum_r,
    go_s,
    go_r,
    x_s,
    x_r,
    f_s,
    f_r,
    half_s,
    half_r,
    side_s,
    side_r,
    back_s,
    back_r,
    mix_s,
    mix_r,
):
    ny, nz = split
    chips = ny * nz
    half = ny // 2
    c, p, t, y, z, device = places(split, tensors)
    tokens, quarter = x_ref.shape
    full = quarter * tensors
    rows, width = wbuf.shape[2:]
    per_quarter = quarter // rows
    slots = 2 * CAP
    all_slots = chips * slots
    hidden_width = gate.shape[1]
    right, left = 0, 1
    signs = (1, -1)

    dense_loads = [
        pltpu.make_async_copy(far, dense_held.at[m], load_sem.at[m])
        for m, far in enumerate((dense_gate_hbm, dense_up_hbm, dense_down_hbm))
    ]
    dense_loads.append(pltpu.make_async_copy(x_hbm, x_ref, load_sem.at[3]))
    expert_loads = [
        pltpu.make_async_copy(far.at[c], near, load_sem.at[4 + i])
        for i, (far, near) in enumerate(((gate_hbm, gate), (up_hbm, up), (down_hbm, down)))
    ]
    for load in dense_loads + expert_loads:
        load.start()

    group = [(dy, dt) for dt in range(tensors) for dy in range(ny) if dy or dt]
    others = [(dc, dt) for dc in range(2) for dt in range(tensors) if dc or dt]
    offsets = {(0, dy, 0, dt) for dy, dt in group}
    offsets |= {(dc, 0, 0, dt) for dc, dt in others}
    offsets |= {(0, dy, dz, 0) for dy in range(ny) for dz in range(nz) if dy or dz}
    greet(sorted(offsets), device)
    for load in dense_loads:
        load.wait()

    started = []

    def send(src, dst, send_sem, recv_sem, to, keep=True):
        copy = pltpu.make_async_remote_copy(
            src_ref=src,
            dst_ref=dst,
            send_sem=send_sem,
            recv_sem=recv_sem,
            device_id=to,
            device_id_type=MESH,
        )
        copy.start()
        if keep:
            started.append(copy)

    def first_hop(m):
        copies = []
        for dy in range(1, ny):
            there = lax.rem(y + dy, ny)
            columns = pl.ds(pl.multiple_of(there * width, 128), width)
            copies.append(
                pltpu.make_async_remote_copy(
                    src_ref=dense_held.at[m, :, columns],
                    dst_ref=wbuf.at[p, m],
                    send_sem=w1_s.at[dy - 1, m],
                    recv_sem=w1_r.at[lax.rem(y, half), m],
                    device_id=device(0, dy, 0, 0),
                    device_id_type=MESH,
                )
            )
        return copies

    sends_weights = y // half == c

    @pl.when(sends_weights)
    def _():
        for m in range(3):
            for copy in first_hop(m):
                copy.start()
            columns = pl.ds(pl.multiple_of(y * width, 128), width)
            pltpu.make_async_copy(
                dense_held.at[m, :, columns], wbuf.at[p, m], w1_r.at[lax.rem(y, half), m]
            ).start()

    kinds = (pl.ds(0, 2), pl.ds(2, 1))
    hops = {}
    for a in range(half):
        far, near = nz // 2, (nz - 1) // 2
        hops[right, a], hops[left, a] = (far, near) if a % 2 == 0 else (near, far)

    def piece(core, a, dz):
        return (half * core + a) * nz + lax.rem(z + dz + nz, nz)

    def forward(kind, a, direction, step):
        sign = signs[direction]
        held = wbuf.at[piece(c, a, -sign * (step - 1)), kinds[kind]]
        send(
            held,
            held,
            ring_s.at[kind, direction, a, step - 1],
            ring_r.at[kind, direction, a, step - 1],
            device(0, 0, sign % nz, 0),
        )

    def hand_over(kind, a, dz):
        held = wbuf.at[piece(c, a, dz), kinds[kind]]
        send(held, held, sib_s.at[kind, a, dz % nz], sib_r.at[kind, a, dz % nz], device(1, 0, 0, 0))

    def begin(kind, a):
        for m in range(2) if kind == 0 else (2,):
            wait_bytes(wbuf.at[piece(c, a, 0), m], w1_r.at[a, m])
        for direction in (right, left):
            if hops[direction, a] >= 1:
                forward(kind, a, direction, 1)
        hand_over(kind, a, 0)

    def ring(kind, a, step):
        for direction in (right, left):
            if step > hops[direction, a]:
                continue
            sign = signs[direction]
            wait_bytes(
                wbuf.at[piece(c, a, -sign * step), kinds[kind]],
                ring_r.at[kind, direction, a, step - 1],
            )
            if step + 1 <= hops[direction, a]:
                forward(kind, a, direction, step + 1)
            hand_over(kind, a, -sign * step)

    def from_other_core(kind, a):
        for dz in range(nz):
            wait_bytes(wbuf.at[piece(1 - c, a, dz), kinds[kind]], sib_r.at[kind, a, dz])

    for a in range(half):
        begin(0, a)

    for i, (dy, dt) in enumerate(group):
        send(x_ref, xbuf.at[t, y], tok_s.at[i], tok_r.at[i], device(0, dy, 0, dt))
    xbuf[t, y] = x_ref[...]

    def expert_at(k):
        there = lax.rem(y + k // nz, ny) * nz + lax.rem(z + k % nz, nz)
        return 2 * there + c

    def iotas(shape):
        return (lax.broadcasted_iota(jnp.int32, shape, i) for i in range(2))

    def plan_routes():
        experts = expert_at(lax.broadcasted_iota(jnp.int32, (chips, tokens), 0))
        one, two = iotas((tokens, tokens))
        before = jnp.where(one < two, 1.0, 0.0).astype(jnp.bfloat16)
        slot, chip = iotas((all_slots, chips))
        spread_t = jnp.where(slot // slots == chip, 1.0, 0.0).astype(jnp.bfloat16)
        chip, slot = iotas((chips, all_slots))
        spread = jnp.where(slot // slots == chip, 1.0, 0.0).astype(jnp.bfloat16)

        def chosen(found, slot, m):
            rank = jnp.where((slot // CAP) % 2 == m, slot % CAP, 2 * tokens)
            return found == rank.astype(jnp.float32)

        for m in range(2):
            named = jnp.zeros((chips, tokens), jnp.float32)
            share = jnp.zeros((chips, tokens), jnp.float32)
            for j in range(ids_ref.shape[0]):
                same = ids_ref[j, m : m + 1, :] == experts
                named += jnp.where(same, 1.0, 0.0)
                share += jnp.where(same, route_ref[j, m : m + 1, :], 0.0)
            ranks = jnp.dot(
                named.astype(jnp.bfloat16), before, preferred_element_type=jnp.float32
            )
            ranks = jnp.where(named > 0.5, ranks, -1.0)
            found = jnp.dot(
                spread_t, ranks.astype(jnp.bfloat16), preferred_element_type=jnp.float32
            )
            slot, token = iotas((all_slots, tokens))
            place[m] = jnp.where(chosen(found, slot, m), 1.0, 0.0).astype(jnp.bfloat16)
            ranks_t, share_t = ranks.T, share.T
            found = jnp.dot(
                ranks_t.astype(jnp.bfloat16), spread, preferred_element_type=jnp.float32
            )
            token, slot = iotas((tokens, all_slots))
            here = chosen(found, slot, m)
            high = share_t.astype(jnp.bfloat16)
            low = (share_t - high.astype(jnp.float32)).astype(jnp.bfloat16)
            for i, values in enumerate((high, low)):
                values = jnp.dot(values, spread, preferred_element_type=jnp.float32)
                mixers[m, i] = jnp.where(here, values, 0.0).astype(jnp.bfloat16)

    def norm_block(j, carry):
        squares = jnp.zeros((tokens, 1), jnp.float32)
        for q in range(tensors):
            values = xbuf[q, j].astype(jnp.float32)
            squares += jnp.sum(values * values, axis=1, keepdims=True)
        inverse = lax.rsqrt(squares / full + EPSILON)
        for q in range(tensors):
            values = xbuf[q, j].astype(jnp.float32)
            gain = gain_dense_ref[q * quarter : (q + 1) * quarter].reshape(1, quarter)
            xbuf[q, j] = (values * inverse * gain).astype(jnp.bfloat16)
        return carry

    def make_hidden():
        gate_sums = jnp.zeros((ny * tokens, width), jnp.float32)
        upward = jnp.zeros((ny * tokens, width), jnp.float32)
        for q in range(tensors):
            normed = xbuf[q].reshape(ny * tokens, quarter)
            held = pl.ds(q * per_quarter, per_quarter)
            gate_sums += jnp.dot(
                normed, wbuf[held, 0].reshape(quarter, width), preferred_element_type=jnp.float32
            )
            upward += jnp.dot(
                normed, wbuf[held, 1].reshape(quarter, width), preferred_element_type=jnp.float32
            )
        hidden_ref[...] = (silu(gate_sums) * upward).astype(jnp.bfloat16)

    def give_quarter(q):
        held = wbuf[pl.ds(q * per_quarter, per_quarter), 2].reshape(quarter, width)
        result = lax.dot_general(
            hidden_ref[...], held, (((1,), (1,)), ((), ())), preferred_element_type=jnp.float32
        )
        part[q] = result.astype(jnp.bfloat16).reshape(ny, tokens, quarter)
        dt = lax.rem(q - t + tensors, tensors)
        for dy in [*range(1, ny), 0]:

            def go(dy=dy):
                at = dy * tensors + dt
                send(
                    part.at[q, lax.rem(y + dy, ny)],
                    prec.at[at],
                    out_s.at[at],
                    out_r.at[at],
                    device(0, dy, 0, dt),
                    keep=False,
                )

            if dy:
                go()
            else:
                pl.when(dt > 0)(go)

    def quarters(a):
        return [q for q in range(tensors) if (q * per_quarter // nz) % half == a]

    steps = nz // 2
    for step in range(1, steps + 1):
        for a in range(half):
            ring(0, a, step)
        if step == 1:
            plan_routes()
            for i in range(len(group)):
                wait_bytes(xbuf.at[0, 0], tok_r.at[i])
            lax.fori_loop(0, ny, norm_block, 0)
        if step == max(steps - 1, 1):
            begin(1, 0)
        if step == steps and half > 1:
            begin(1, half - 1)
    for step in range(1, steps + 1):
        ring(1, 0, step)
        if step == 1:
            for a in range(half):
                from_other_core(0, a)
            make_hidden()
        if half > 1 and step < steps:
            ring(1, half - 1, step)
    from_other_core(1, 0)
    if half == 1:
        for q in range(tensors):
            give_quarter(q)
    else:
        for q in quarters(0):
            give_quarter(q)
        ring(1, half - 1, steps)
        from_other_core(1, half - 1)
        for q in quarters(half - 1):
            give_quarter(q)

    total = part[t, y].astype(jnp.float32)
    for dy, dt in group:
        wait_bytes(prec.at[dy * tensors + dt], out_r.at[dy * tensors + dt])
        total += prec[dy * tensors + dt].astype(jnp.float32)
    own = (x_ref[...].astype(jnp.float32) + total).astype(jnp.bfloat16)

    mids[c] = own
    wide = own.astype(jnp.float32)
    sums[t, c] = jnp.broadcast_to(jnp.sum(wide * wide, axis=1, keepdims=True), (tokens, 128))
    for i, (dc, dt) in enumerate(others):
        send(sums.at[t, c], sums.at[t, c], sum_s.at[i], sum_r.at[i], device(dc, 0, 0, dt))
    send(mids.at[c], mids.at[c], mid_s, mid_r, device(1, 0, 0, 0))
    wait_bytes(mids.at[0], mid_r)
    for i in range(len(others)):
        wait_bytes(sums.at[0, 0], sum_r.at[i])
    normed = []
    gain = gain_expert_ref[pl.ds(pl.multiple_of(t * quarter, 128), quarter)].reshape(1, quarter)
    for m in range(2):
        squares = sums[0, m]
        for q in range(1, tensors):
            squares += sums[q, m]
        inverse = lax.rsqrt(squares[:, :1] / full + EPSILON)
        normed.append((mids[m].astype(jnp.float32) * inverse * gain).astype(jnp.bfloat16))

    for dy in range(ny):
        these = pl.ds(dy * nz * slots, nz * slots)
        block = jnp.dot(place[0, these], normed[0], preferred_element_type=jnp.float32)
        block += jnp.dot(place[1, these], normed[1], preferred_element_type=jnp.float32)
        block = block.reshape(nz, slots, quarter).astype(jnp.bfloat16)
        outgoing[pl.ds(dy * nz, nz)] = block
        if dy == 0:
            arrived[t, 0] = block[0]

        def go(dz, carry, dy=dy):
            k = dy * nz + dz
            send(
                outgoing.at[k],
                arrived.at[t, k],
                go_s.at[k],
                go_r.at[k],
                device(0, dy, dz, 0),
                keep=False,
            )
            return carry

        lax.fori_loop(1 if dy == 0 else 0, nz, go, 0)

    for load in expert_loads:
        load.wait()

    cut = nz // 2
    ways = ((right, 1), (left, tensors - 1))
    far_away = tensors // 2

    def some(chunk):
        return pl.ds(chunk * nz, nz)

    def half_of(chunk, way):
        return pl.ds(chunk * nz + way * cut, cut)

    def share_chunk(chunk):
        def arrive(dz, carry):
            k = chunk * nz + dz

            @pl.when(k > 0)
            def _():
                wait_bytes(arrived.at[t, k], go_r.at[k])

            return carry

        lax.fori_loop(0, nz, arrive, 0)
        held = arrived.at[t, some(chunk)]
        for way, dt in ways:
            send(held, held, x_s.at[way, chunk], x_r.at[way, chunk], device(0, 0, 0, dt), False)

    def forward_chunk(chunk):
        for way, dt in ways:
            source = lax.rem(t + tensors - dt, tensors)
            wait_bytes(arrived.at[source, some(chunk)], x_r.at[way, chunk])
            held = arrived.at[source, half_of(chunk, way)]
            send(held, held, f_s.at[way, chunk], f_r.at[way, chunk], device(0, 0, 0, dt), False)

    def compute_chunk(chunk):
        here = some(chunk)
        source = lax.rem(t + far_away, tensors)
        for way, dt in ways:
            wait_bytes(arrived.at[source, half_of(chunk, way)], f_r.at[way, chunk])
        gate_sums = jnp.zeros((nz * slots, hidden_width), jnp.float32)
        upward = jnp.zeros((nz * slots, hidden_width), jnp.float32)
        for q in range(tensors):
            values = arrived[q, here].reshape(nz * slots, quarter)
            these = slice(q * quarter, (q + 1) * quarter)
            gate_sums += jnp.dot(values, gate[these], preferred_element_type=jnp.float32)
            upward += jnp.dot(values, up[these], preferred_element_type=jnp.float32)
        hidden = (silu(gate_sums) * upward).astype(jnp.bfloat16)
        for dt in (far_away, 1, tensors - 1, 0):
            there = lax.rem(t + dt, tensors)
            columns = pl.ds(pl.multiple_of(there * quarter, 128), quarter)
            result = jnp.dot(hidden, down[:, columns], preferred_element_type=jnp.float32)
            pieces[dt, here] = result.reshape(nz, slots, quarter).astype(jnp.bfloat16)
            if dt == far_away:
                for way, near in ways:
                    send(
                        pieces.at[dt, half_of(chunk, way)],
                        through.at[way, pl.ds(chunk * cut, cut)],
                        half_s.at[way, chunk],
                        half_r.at[way, chunk],
                        device(0, 0, 0, near),
                        False,
                    )

    def relay_chunk(chunk):
        for way, dt in ways:
            came = pl.ds(chunk * cut, cut)
            wait_bytes(through.at[way, came], half_r.at[way, chunk])
            these = half_of(chunk, way)
            both = pieces[dt, these].astype(jnp.float32) + through[way, came].astype(jnp.float32)
            pieces[dt, these] = both.astype(jnp.bfloat16)
            send(
                pieces.at[dt, some(chunk)],
                beside.at[way, some(chunk)],
                side_s.at[way, chunk],
                side_r.at[way, chunk],
                device(0, 0, 0, dt),
                False,
            )

    def return_chunk(chunk):
        here = some(chunk)
        total = pieces[0, here].astype(jnp.float32)
        for way, dt in ways:
            wait_bytes(beside.at[way, here], side_r.at[way, chunk])
            total += beside[way, here].astype(jnp.float32)
        summed[here] = total.astype(jnp.bfloat16)

        def give(dz, carry):
            k = chunk * nz + dz

            @pl.when(k > 0)
            def _():
                send(
                    summed.at[k],
                    returned.at[k],
                    back_s.at[k],
                    back_r.at[k],
                    device(0, ny - chunk, nz - dz, 0),
                    False,
                )

            return carry

        lax.fori_loop(0, nz, give, 0)

    work = (share_chunk, forward_chunk, compute_chunk, relay_chunk, return_chunk)

    def stage(i, carry):
        for lag, act in enumerate(work):

            @pl.when((i >= lag) & (i < ny + lag))
            def _(lag=lag, act=act):
                act(i - lag)

        return carry

    lax.fori_loop(0, ny + len(work) - 1, stage, 0)
    returned[0] = summed[0]

    def arrive_back(k, carry):
        wait_bytes(returned.at[k], back_r.at[k])
        return carry

    lax.fori_loop(1, chips, arrive_back, 0)
    back = returned[...].reshape(all_slots, quarter)
    for m in range(2):
        mixed = jnp.dot(mixers[m, 0], back, preferred_element_type=jnp.float32)
        mixed += jnp.dot(mixers[m, 1], back, preferred_element_type=jnp.float32)
        mixes[0, m] = mixed
    send(mixes.at[0], mixes.at[1], mix_s, mix_r, device(1, 0, 0, 0))
    wait_bytes(mixes.at[1], mix_r)
    for m in range(2):
        first = mids[m]
        final = first.astype(jnp.float32) + (mixes[0, m] + mixes[1, m])
        out_ref[m] = jnp.where(c == 0, first, final.astype(jnp.bfloat16))

    for copy in started:
        copy.wait_send()
    for dy, dt in group:
        wait_bytes(prec.at[0], out_s.at[dy * tensors + dt])

    @pl.when(sends_weights)
    def _():
        for m in range(3):
            for copy in first_hop(m):
                copy.wait_send()

    def sent(k, carry):
        wait_bytes(outgoing.at[k], go_s.at[k])
        wait_bytes(summed.at[k], back_s.at[k])
        return carry

    lax.fori_loop(1, chips, sent, 0)

    def sent_chunk(chunk, carry):
        for way, dt in ways:
            wait_bytes(arrived.at[0, some(chunk)], x_s.at[way, chunk])
            wait_bytes(arrived.at[0, half_of(chunk, way)], f_s.at[way, chunk])
            wait_bytes(arrived.at[0, half_of(chunk, way)], half_s.at[way, chunk])
            wait_bytes(pieces.at[0, some(chunk)], side_s.at[way, chunk])
        return carry

    lax.fori_loop(0, ny, sent_chunk, 0)


def body(
    split,
    tensors,
    activations,
    expert_ids,
    route_weights,
    gain_dense,
    gain_expert,
    dense_gate,
    dense_up,
    dense_down,
    expert_gate,
    expert_up,
    expert_down,
):
    ny, nz = split
    chips = ny * nz
    half = ny // 2
    tokens, quarter = activations.shape[1:]
    full = quarter * tensors
    rows, dense_hidden = dense_gate.shape
    width = dense_hidden // ny
    slots = 2 * CAP
    hidden = expert_gate.shape[2]
    group = ny * tensors - 1
    steps = nz // 2
    bf16, f32 = jnp.bfloat16, jnp.float32
    dma = pltpu.SemaphoreType.DMA
    vmem = pl.BlockSpec(memory_space=pltpu.VMEM)
    hbm = pl.BlockSpec(memory_space=pl.ANY)
    sent_rows = (chips, slots, quarter)
    sections = pl.pallas_call(
        functools.partial(kernel, split, tensors),
        out_shape=jax.ShapeDtypeStruct((2, tokens, quarter), bf16),
        in_specs=[hbm] + [vmem] * 4 + [hbm] * 6,
        out_specs=vmem,
        scratch_shapes=[
            pltpu.VMEM((tokens, quarter), bf16),
            pltpu.VMEM((3, rows, dense_hidden), bf16),
            pltpu.VMEM((tensors, ny, tokens, quarter), bf16),
            pltpu.VMEM((chips, 3, rows, width), bf16),
            pltpu.VMEM((ny * tokens, width), bf16),
            pltpu.VMEM((tensors, ny, tokens, quarter), bf16),
            pltpu.VMEM((ny * tensors, tokens, quarter), bf16),
            pltpu.VMEM((full, hidden), bf16),
            pltpu.VMEM((full, hidden), bf16),
            pltpu.VMEM((hidden, full), bf16),
            pltpu.VMEM((2, chips * slots, tokens), bf16),
            pltpu.VMEM((2, 2, tokens, chips * slots), bf16),
            pltpu.VMEM((2, tokens, quarter), bf16),
            pltpu.VMEM((tensors, 2, tokens, 128), f32),
            pltpu.VMEM(sent_rows, bf16),
            pltpu.VMEM((tensors, *sent_rows), bf16),
            pltpu.VMEM((tensors, *sent_rows), bf16),
            pltpu.VMEM((2, chips // 2, slots, quarter), bf16),
            pltpu.VMEM((2, *sent_rows), bf16),
            pltpu.VMEM(sent_rows, bf16),
            pltpu.VMEM(sent_rows, bf16),
            pltpu.VMEM((2, 2, tokens, quarter), f32),
            dma((7,)),
            dma((group,)),
            dma((group,)),
            dma((ny - 1, 3)),
            dma((half, 3)),
            dma((2, 2, half, steps)),
            dma((2, 2, half, steps)),
            dma((2, half, nz)),
            dma((2, half, nz)),
            dma((ny * tensors,)),
            dma((ny * tensors,)),
            dma(()),
            dma(()),
            dma((2 * tensors - 1,)),
            dma((2 * tensors - 1,)),
            dma((chips,)),
            dma((chips,)),
            dma((2, ny)),
            dma((2, ny)),
            dma((2, ny)),
            dma((2, ny)),
            dma((2, ny)),
            dma((2, ny)),
            dma((2, ny)),
            dma((2, ny)),
            dma((chips,)),
            dma((chips,)),
            dma(()),
            dma(()),
        ],
        compiler_params=pltpu.CompilerParams(
            collective_id=0, has_side_effects=True, vmem_limit_bytes=58 * 2**20
        ),
        name="sections",
    )(
        activations[0],
        expert_ids.transpose(2, 0, 1),
        route_weights.transpose(2, 0, 1),
        gain_dense,
        gain_expert,
        dense_gate,
        dense_up,
        dense_down,
        expert_gate,
        expert_up,
        expert_down,
    )
    return sections[None]


def solution(mesh, split=SPLIT):
    placed = (
        P("segment", "expert", "tensor"),
        P(None, "expert", None),
        P(None, "expert", None),
        P(),
        P(),
        P("expert", "tensor"),
        P("expert", "tensor"),
        P("expert", "tensor"),
        P("expert", None, "tensor"),
        P("expert", None, "tensor"),
        P("expert", "tensor", None),
    )
    return jax.shard_map(
        functools.partial(body, split, mesh.shape["tensor"]),
        mesh=mesh,
        in_specs=placed,
        out_specs=P("segment", None, "expert", "tensor"),
        check_vma=False,
    )
```

time: 640 us -> 182 us (0.28)
  waiting for transfers between devices: 391 us -> 0 us
  Pallas kernels: 0 us -> 181 us
  blocking collectives: 77.7 us -> 0 us
  local copies, waits for them, and re-layouts: 77.5 us -> 1.6 us
  matrix products: 46.4 us -> 0 us
  starting transfers between devices: 22.2 us -> 0 us
  between operations: 13.9 us -> 0.01 us
  other arithmetic: 6.87 us -> 0 us
    all_gather x5 -> x0, waiting for transfers between devices: 302 us -> none  [the longest x1 95.6 us: dense_folded(): lax.all_gather(dense_up, 'expert', axis=0, tiled=True)]
    pallas_call x0 -> x1, Pallas kernels: none -> 181 us  [body(): pl.pallas_call(functools.partial(kernel, split, tensors), out_shape=jax.S...]
    unnamed x11 -> x0, waiting for transfers between devices: 71.2 us -> none
    all_to_all x2 -> x0, blocking collectives: 59.8 us -> none  [expert_block(): lax.all_to_all(outgoing, 'expert', split_axis=1, concat_axis=1, tiled=True)]
    dot_general x6 -> x0, matrix products: 46.4 us -> none  [the longest x2 21.3 us: expert_block(): jnp.einsum('lrh,lhd->lrd', hidden, expert_down, preferred_element_type=jn...]
    unnamed x30 -> x1, local copies, waits for them, and re-layouts: 40.2 us -> 1.6 us
    all_to_all x2 -> x0, starting transfers between devices: 19.3 us -> none  [expert_block(): lax.all_to_all(summed.reshape(local_count, groups, capacity, quarter), 'e...]
    all_to_all x2 -> x0, waiting for transfers between devices: 17.1 us -> none  [expert_block(): lax.all_to_all(summed.reshape(local_count, groups, capacity, quarter), 'e...]
  transfers between devices with their start and end apart: 11 -> 0, of which waited for: 10 -> 0; matrix products, arithmetic and copies ran while one was open for 16% -> 0% of each run, Pallas kernels for 0% -> 0%
where the time goes in v2:
time: 182 us
  Pallas kernels  181 us (99%)
    pallas_call x1, Pallas kernels, body(): pl.pallas_call(functools.partial(kernel, split, tensors), out_shape=jax.S...  181 us

profile of v2, /device:TPU:1, one launch (start us, length us, event | category | flops | bytes accessed | tf_op | source)
XLA Modules:
  0.0 182.2 jit_solution(6053130970286807359)
XLA Ops:
  0.0 180.6 %sections.1 = bf16[2,64,640]{2,1,0:T(8,128)(2,1)} custom-call(bf16[64,640]{1,0:T(8,128)(2,1)} %bitcast.5, s32[6,2,64]{2,1,0:T(2,128)} %bitcast.6, f32[6,2,64]{2,1,0:T(2,128)} %bitcast.7, f32[2560]{0:T(1024)} %gain_dense_ref.1, f32[2560]{0:T(1024)} %gain_expert_ref.1, bf16[80,1536]{1,0:T(8,128)(2,1)} %dense_gate_hbm.1, bf16[80,1536]{1,0:T(8,128)(2,1)} %dense_up_hbm.1, ...), custom_call_target="tpu_custom_call" | custom-call | tf_op jit(solution)/shard_map/sections/pallas_call | solution.py:627
  180.6 1.6 copy.13

commit v3 on v2

--- a/solution.py
+++ b/solution.py
@@ -10,6 +10,7 @@
 EPSILON = 1e-06
 MESH = pl.DeviceIdType.MESH
 CAP = 12
+CHUNKS = 8
 SPLIT = (4, 8)
 
 
@@ -64,7 +65,12 @@
     wbuf,
     hidden_ref,
     part,
-    prec,
+    along_x,
+    along_y,
+    over_x,
+    over_y,
+    last_y,
+    last_x,
     gate,
     up,
     down,
@@ -89,8 +95,14 @@
     ring_r,
     sib_s,
     sib_r,
-    out_s,
-    out_r,
+    a1_s,
+    a1_r,
+    b1_s,
+    b1_r,
+    a2_s,
+    a2_r,
+    b2_s,
+    b2_r,
     mid_s,
     mid_r,
     sum_s,
@@ -123,6 +135,7 @@
     hidden_width = gate.shape[1]
     right, left = 0, 1
     signs = (1, -1)
+    first, second = pl.ds(0, tokens // 2), pl.ds(tokens // 2, tokens // 2)
 
     dense_loads = [
         pltpu.make_async_copy(far, dense_held.at[m], load_sem.at[m])
@@ -305,19 +318,15 @@
             xbuf[q, j] = (values * inverse * gain).astype(jnp.bfloat16)
         return carry
 
-    def make_hidden():
-        gate_sums = jnp.zeros((ny * tokens, width), jnp.float32)
-        upward = jnp.zeros((ny * tokens, width), jnp.float32)
-        for q in range(tensors):
-            normed = xbuf[q].reshape(ny * tokens, quarter)
-            held = pl.ds(q * per_quarter, per_quarter)
-            gate_sums += jnp.dot(
-                normed, wbuf[held, 0].reshape(quarter, width), preferred_element_type=jnp.float32
-            )
-            upward += jnp.dot(
-                normed, wbuf[held, 1].reshape(quarter, width), preferred_element_type=jnp.float32
-            )
-        hidden_ref[...] = (silu(gate_sums) * upward).astype(jnp.bfloat16)
+    acc = [jnp.zeros((ny * tokens, width), jnp.float32) for _ in range(2)]
+
+    def add_quarter(q):
+        normed = xbuf[q].reshape(ny * tokens, quarter)
+        held = pl.ds(q * per_quarter, per_quarter)
+        for i in range(2):
+            acc[i] += jnp.dot(
+                normed, wbuf[held, i].reshape(quarter, width), preferred_element_type=jnp.float32
+            )
 
     def give_quarter(q):
         held = wbuf[pl.ds(q * per_quarter, per_quarter), 2].reshape(quarter, width)
@@ -325,65 +334,101 @@
             hidden_ref[...], held, (((1,), (1,)), ((), ())), preferred_element_type=jnp.float32
         )
         part[q] = result.astype(jnp.bfloat16).reshape(ny, tokens, quarter)
+        for dy in range(1, ny):
+            send(
+                part.at[q, lax.rem(y + dy, ny), second],
+                along_y.at[dy - 1, q],
+                b1_s.at[dy - 1, q],
+                b1_r.at[dy - 1, q],
+                device(0, dy, 0, 0),
+                keep=False,
+            )
         dt = lax.rem(q - t + tensors, tensors)
-        for dy in [*range(1, ny), 0]:
-
-            def go(dy=dy):
-                at = dy * tensors + dt
-                send(
-                    part.at[q, lax.rem(y + dy, ny)],
-                    prec.at[at],
-                    out_s.at[at],
-                    out_r.at[at],
-                    device(0, dy, 0, dt),
-                    keep=False,
-                )
-
-            if dy:
-                go()
-            else:
-                pl.when(dt > 0)(go)
+
+        @pl.when(dt > 0)
+        def _():
+            send(
+                part.at[q, :, first],
+                along_x.at[dt - 1],
+                a1_s.at[dt - 1],
+                a1_r.at[dt - 1],
+                device(0, 0, 0, dt),
+                keep=False,
+            )
 
     def quarters(a):
-        return [q for q in range(tensors) if (q * per_quarter // nz) % half == a]
+        last = [((q + 1) * per_quarter - 1) // nz % half for q in range(tensors)]
+        return [q for q in range(tensors) if last[q] == a]
 
     steps = nz // 2
+    early = max(steps - 1, 1)
     for step in range(1, steps + 1):
         for a in range(half):
             ring(0, a, step)
-        if step == 1:
-            plan_routes()
+        if step == early:
+            begin(1, 0)
             for i in range(len(group)):
                 wait_bytes(xbuf.at[0, 0], tok_r.at[i])
             lax.fori_loop(0, ny, norm_block, 0)
-        if step == max(steps - 1, 1):
-            begin(1, 0)
         if step == steps and half > 1:
             begin(1, half - 1)
+    left_over = list(range(tensors))
     for step in range(1, steps + 1):
         ring(1, 0, step)
+        if half > 1 and step < steps:
+            ring(1, half - 1, step)
         if step == 1:
             for a in range(half):
                 from_other_core(0, a)
-            make_hidden()
-        if half > 1 and step < steps:
-            ring(1, half - 1, step)
-    from_other_core(1, 0)
-    if half == 1:
+        if step < steps and left_over:
+            add_quarter(left_over.pop(0))
+    for q in left_over:
+        add_quarter(q)
+    hidden_ref[...] = (silu(acc[0]) * acc[1]).astype(jnp.bfloat16)
+    for a in range(half):
+        if a:
+            ring(1, a, steps)
+        from_other_core(1, a)
+        for q in quarters(a):
+            give_quarter(q)
+    plan_routes()
+
+    total = part[t, :, first].astype(jnp.float32)
+    for i in range(tensors - 1):
+        wait_bytes(along_x.at[i], a1_r.at[i])
+        total += along_x[i].astype(jnp.float32)
+    over_x[...] = total.astype(jnp.bfloat16)
+    for dy in range(1, ny):
+        send(
+            over_x.at[lax.rem(y + dy, ny)],
+            last_y.at[dy - 1],
+            a2_s.at[dy - 1],
+            a2_r.at[dy - 1],
+            device(0, dy, 0, 0),
+        )
+    total = part[:, y, second].astype(jnp.float32)
+    for dy in range(1, ny):
         for q in range(tensors):
-            give_quarter(q)
-    else:
-        for q in quarters(0):
-            give_quarter(q)
-        ring(1, half - 1, steps)
-        from_other_core(1, half - 1)
-        for q in quarters(half - 1):
-            give_quarter(q)
-
-    total = part[t, y].astype(jnp.float32)
-    for dy, dt in group:
-        wait_bytes(prec.at[dy * tensors + dt], out_r.at[dy * tensors + dt])
-        total += prec[dy * tensors + dt].astype(jnp.float32)
+            wait_bytes(along_y.at[dy - 1, q], b1_r.at[dy - 1, q])
+        total += along_y[dy - 1].astype(jnp.float32)
+    over_y[...] = total.astype(jnp.bfloat16)
+    for dt in range(1, tensors):
+        send(
+            over_y.at[lax.rem(t + dt, tensors)],
+            last_x.at[dt - 1],
+            b2_s.at[dt - 1],
+            b2_r.at[dt - 1],
+            device(0, 0, 0, dt),
+        )
+    upper = over_x[y].astype(jnp.float32)
+    for dy in range(1, ny):
+        wait_bytes(last_y.at[dy - 1], a2_r.at[dy - 1])
+        upper += last_y[dy - 1].astype(jnp.float32)
+    lower = over_y[t].astype(jnp.float32)
+    for dt in range(1, tensors):
+        wait_bytes(last_x.at[dt - 1], b2_r.at[dt - 1])
+        lower += last_x[dt - 1].astype(jnp.float32)
+    total = jnp.concatenate([upper, lower], axis=0)
     own = (x_ref[...].astype(jnp.float32) + total).astype(jnp.bfloat16)
 
     mids[c] = own
@@ -404,45 +449,45 @@
         inverse = lax.rsqrt(squares[:, :1] / full + EPSILON)
         normed.append((mids[m].astype(jnp.float32) * inverse * gain).astype(jnp.bfloat16))
 
-    for dy in range(ny):
-        these = pl.ds(dy * nz * slots, nz * slots)
+    per = chips // CHUNKS
+    for chunk in range(CHUNKS):
+        these = pl.ds(chunk * per * slots, per * slots)
         block = jnp.dot(place[0, these], normed[0], preferred_element_type=jnp.float32)
         block += jnp.dot(place[1, these], normed[1], preferred_element_type=jnp.float32)
-        block = block.reshape(nz, slots, quarter).astype(jnp.bfloat16)
-        outgoing[pl.ds(dy * nz, nz)] = block
-        if dy == 0:
+        block = block.reshape(per, slots, quarter).astype(jnp.bfloat16)
+        outgoing[pl.ds(chunk * per, per)] = block
+        if chunk == 0:
             arrived[t, 0] = block[0]
 
-        def go(dz, carry, dy=dy):
-            k = dy * nz + dz
+        def go(k, carry):
             send(
                 outgoing.at[k],
                 arrived.at[t, k],
                 go_s.at[k],
                 go_r.at[k],
-                device(0, dy, dz, 0),
+                device(0, k // nz, k % nz, 0),
                 keep=False,
             )
             return carry
 
-        lax.fori_loop(1 if dy == 0 else 0, nz, go, 0)
+        lax.fori_loop(max(chunk * per, 1), (chunk + 1) * per, go, 0)
 
     for load in expert_loads:
         load.wait()
 
-    cut = nz // 2
+    cut = per // 2
     ways = ((right, 1), (left, tensors - 1))
     far_away = tensors // 2
 
     def some(chunk):
-        return pl.ds(chunk * nz, nz)
+        return pl.ds(chunk * per, per)
 
     def half_of(chunk, way):
-        return pl.ds(chunk * nz + way * cut, cut)
+        return pl.ds(chunk * per + way * cut, cut)
 
     def share_chunk(chunk):
-        def arrive(dz, carry):
-            k = chunk * nz + dz
+        def arrive(i, carry):
+            k = chunk * per + i
 
             @pl.when(k > 0)
             def _():
@@ -450,7 +495,7 @@
 
             return carry
 
-        lax.fori_loop(0, nz, arrive, 0)
+        lax.fori_loop(0, per, arrive, 0)
         held = arrived.at[t, some(chunk)]
         for way, dt in ways:
             send(held, held, x_s.at[way, chunk], x_r.at[way, chunk], device(0, 0, 0, dt), False)
@@ -467,10 +512,10 @@
         source = lax.rem(t + far_away, tensors)
         for way, dt in ways:
             wait_bytes(arrived.at[source, half_of(chunk, way)], f_r.at[way, chunk])
-        gate_sums = jnp.zeros((nz * slots, hidden_width), jnp.float32)
-        upward = jnp.zeros((nz * slots, hidden_width), jnp.float32)
+        gate_sums = jnp.zeros((per * slots, hidden_width), jnp.float32)
+        upward = jnp.zeros((per * slots, hidden_width), jnp.float32)
         for q in range(tensors):
-            values = arrived[q, here].reshape(nz * slots, quarter)
+            values = arrived[q, here].reshape(per * slots, quarter)
             these = slice(q * quarter, (q + 1) * quarter)
             gate_sums += jnp.dot(values, gate[these], preferred_element_type=jnp.float32)
             upward += jnp.dot(values, up[these], preferred_element_type=jnp.float32)
@@ -479,7 +524,7 @@
             there = lax.rem(t + dt, tensors)
             columns = pl.ds(pl.multiple_of(there * quarter, 128), quarter)
             result = jnp.dot(hidden, down[:, columns], preferred_element_type=jnp.float32)
-            pieces[dt, here] = result.reshape(nz, slots, quarter).astype(jnp.bfloat16)
+            pieces[dt, here] = result.reshape(per, slots, quarter).astype(jnp.bfloat16)
             if dt == far_away:
                 for way, near in ways:
                     send(
@@ -515,8 +560,8 @@
             total += beside[way, here].astype(jnp.float32)
         summed[here] = total.astype(jnp.bfloat16)
 
-        def give(dz, carry):
-            k = chunk * nz + dz
+        def give(i, carry):
+            k = chunk * per + i
 
             @pl.when(k > 0)
             def _():
@@ -525,49 +570,57 @@
                     returned.at[k],
                     back_s.at[k],
                     back_r.at[k],
-                    device(0, ny - chunk, nz - dz, 0),
+                    device(0, ny - k // nz, nz - k % nz, 0),
                     False,
                 )
 
             return carry
 
-        lax.fori_loop(0, nz, give, 0)
-
-    work = (share_chunk, forward_chunk, compute_chunk, relay_chunk, return_chunk)
+        lax.fori_loop(0, per, give, 0)
+
+    work = ((0, share_chunk), (1, forward_chunk), (2, compute_chunk), (3, relay_chunk), (4, return_chunk))
 
     def stage(i, carry):
-        for lag, act in enumerate(work):
-
-            @pl.when((i >= lag) & (i < ny + lag))
+        for lag, act in work:
+
+            @pl.when((i >= lag) & (i < CHUNKS + lag))
             def _(lag=lag, act=act):
                 act(i - lag)
 
         return carry
 
-    lax.fori_loop(0, ny + len(work) - 1, stage, 0)
+    lax.fori_loop(0, CHUNKS + len(work) - 1, stage, 0)
     returned[0] = summed[0]
 
     def arrive_back(k, carry):
         wait_bytes(returned.at[k], back_r.at[k])
         return carry
 
-    lax.fori_loop(1, chips, arrive_back, 0)
-    back = returned[...].reshape(all_slots, quarter)
+    mixed = [jnp.zeros((tokens, quarter), jnp.float32) for _ in range(2)]
+    for i in range(2):
+        low, high = i * chips // 2, (i + 1) * chips // 2
+        lax.fori_loop(max(low, 1), high, arrive_back, 0)
+        back = returned[low:high].reshape(all_slots // 2, quarter)
+        for m in range(2):
+            for j in range(2):
+                mixer = mixers[m, j, :, low * slots : high * slots]
+                mixed[m] += jnp.dot(mixer, back, preferred_element_type=jnp.float32)
     for m in range(2):
-        mixed = jnp.dot(mixers[m, 0], back, preferred_element_type=jnp.float32)
-        mixed += jnp.dot(mixers[m, 1], back, preferred_element_type=jnp.float32)
-        mixes[0, m] = mixed
+        mixes[0, m] = mixed[m]
     send(mixes.at[0], mixes.at[1], mix_s, mix_r, device(1, 0, 0, 0))
     wait_bytes(mixes.at[1], mix_r)
     for m in range(2):
-        first = mids[m]
-        final = first.astype(jnp.float32) + (mixes[0, m] + mixes[1, m])
-        out_ref[m] = jnp.where(c == 0, first, final.astype(jnp.bfloat16))
+        middle = mids[m]
+        final = middle.astype(jnp.float32) + (mixes[0, m] + mixes[1, m])
+        out_ref[m] = jnp.where(c == 0, middle, final.astype(jnp.bfloat16))
 
     for copy in started:
         copy.wait_send()
-    for dy, dt in group:
-        wait_bytes(prec.at[0], out_s.at[dy * tensors + dt])
+    for i in range(tensors - 1):
+        wait_bytes(along_x.at[i], a1_s.at[i])
+    for dy in range(ny - 1):
+        for q in range(tensors):
+            wait_bytes(along_y.at[dy, q], b1_s.at[dy, q])
 
     @pl.when(sends_weights)
     def _():
@@ -590,7 +643,7 @@
             wait_bytes(pieces.at[0, some(chunk)], side_s.at[way, chunk])
         return carry
 
-    lax.fori_loop(0, ny, sent_chunk, 0)
+    lax.fori_loop(0, CHUNKS, sent_chunk, 0)
 
 
 def body(
@@ -636,7 +689,12 @@
             pltpu.VMEM((chips, 3, rows, width), bf16),
             pltpu.VMEM((ny * tokens, width), bf16),
             pltpu.VMEM((tensors, ny, tokens, quarter), bf16),
-            pltpu.VMEM((ny * tensors, tokens, quarter), bf16),
+            pltpu.VMEM((tensors - 1, ny, tokens // 2, quarter), bf16),
+            pltpu.VMEM((ny - 1, tensors, tokens // 2, quarter), bf16),
+            pltpu.VMEM((ny, tokens // 2, quarter), bf16),
+            pltpu.VMEM((tensors, tokens // 2, quarter), bf16),
+            pltpu.VMEM((ny - 1, tokens // 2, quarter), bf16),
+            pltpu.VMEM((tensors - 1, tokens // 2, quarter), bf16),
             pltpu.VMEM((full, hidden), bf16),
             pltpu.VMEM((full, hidden), bf16),
             pltpu.VMEM((hidden, full), bf16),
@@ -661,22 +719,28 @@
             dma((2, 2, half, steps)),
             dma((2, half, nz)),
             dma((2, half, nz)),
-            dma((ny * tensors,)),
-            dma((ny * tensors,)),
+            dma((tensors - 1,)),
+            dma((tensors - 1,)),
+            dma((ny - 1, tensors)),
+            dma((ny - 1, tensors)),
+            dma((ny - 1,)),
+            dma((ny - 1,)),
+            dma((tensors - 1,)),
+            dma((tensors - 1,)),
             dma(()),
             dma(()),
             dma((2 * tensors - 1,)),
             dma((2 * tensors - 1,)),
             dma((chips,)),
             dma((chips,)),
-            dma((2, ny)),
-            dma((2, ny)),
-            dma((2, ny)),
-            dma((2, ny)),
-            dma((2, ny)),
-            dma((2, ny)),
-            dma((2, ny)),
-            dma((2, ny)),
+            dma((2, CHUNKS)),
+            dma((2, CHUNKS)),
+            dma((2, CHUNKS)),
+            dma((2, CHUNKS)),
+            dma((2, CHUNKS)),
+            dma((2, CHUNKS)),
+            dma((2, CHUNKS)),
+            dma((2, CHUNKS)),
             dma((chips,)),
             dma((chips,)),
             dma(()),

time: 182 us -> 165 us (0.907)
  Pallas kernels: 181 us -> 163 us
    pallas_call x1, Pallas kernels: 181 us -> 163 us  [body(): pl.pallas_call(functools.partial(kernel, split, tensors), out_shape=jax.S...]
where the time goes in v3:
time: 165 us
  Pallas kernels  163 us (99%)
    pallas_call x1, Pallas kernels, body(): pl.pallas_call(functools.partial(kernel, split, tensors), out_shape=jax.S...  163 us

profile of v3, /device:TPU:1, one launch (start us, length us, event | category | flops | bytes accessed | tf_op | source)
XLA Modules:
  0.0 164.6 jit_solution(10730086029075164235)
XLA Ops:
  0.0 163.0 %sections.1 = bf16[2,64,640]{2,1,0:T(8,128)(2,1)} custom-call(bf16[64,640]{1,0:T(8,128)(2,1)} %bitcast.5, s32[6,2,64]{2,1,0:T(2,128)} %bitcast.6, f32[6,2,64]{2,1,0:T(2,128)} %bitcast.7, f32[2560]{0:T(1024)} %gain_dense_ref.1, f32[2560]{0:T(1024)} %gain_expert_ref.1, bf16[80,1536]{1,0:T(8,128)(2,1)} %dense_gate_hbm.1, bf16[80,1536]{1,0:T(8,128)(2,1)} %dense_up_hbm.1, ...), custom_call_target="tpu_custom_call" | custom-call | tf_op jit(solution)/shard_map/sections/pallas_call | solution.py:680
  163.0 1.6 copy.13

commit v4 on v3

--- a/solution.py
+++ b/solution.py
@@ -10,7 +10,6 @@
 EPSILON = 1e-06
 MESH = pl.DeviceIdType.MESH
 CAP = 12
-CHUNKS = 8
 SPLIT = (4, 8)
 
 
@@ -77,7 +76,6 @@
     place,
     mixers,
     mids,
-    sums,
     outgoing,
     arrived,
     pieces,
@@ -105,8 +103,6 @@
     b2_r,
     mid_s,
     mid_r,
-    sum_s,
-    sum_r,
     go_s,
     go_r,
     x_s,
@@ -258,8 +254,20 @@
         send(x_ref, xbuf.at[t, y], tok_s.at[i], tok_r.at[i], device(0, dy, 0, dt))
     xbuf[t, y] = x_ref[...]
 
+    per = nz // 2
+    chunks = 2 * ny
+    self_k = chips - per
+
+    def offset(k):
+        chunk = k // per
+        dy = (chunk // 2 + 1) % ny
+        i = (chunk + chunk // (chunks - 2)) % 2 * per + k % per
+        dz = i % 2 * ((i + 1) // 2) + (i + 1) % 2 * ((nz - i // 2) % nz)
+        return dy, dz
+
     def expert_at(k):
-        there = lax.rem(y + k // nz, ny) * nz + lax.rem(z + k % nz, nz)
+        dy, dz = offset(k)
+        there = (y + dy) % ny * nz + (z + dz) % nz
         return 2 * there + c
 
     def iotas(shape):
@@ -271,8 +279,6 @@
         before = jnp.where(one < two, 1.0, 0.0).astype(jnp.bfloat16)
         slot, chip = iotas((all_slots, chips))
         spread_t = jnp.where(slot // slots == chip, 1.0, 0.0).astype(jnp.bfloat16)
-        chip, slot = iotas((chips, all_slots))
-        spread = jnp.where(slot // slots == chip, 1.0, 0.0).astype(jnp.bfloat16)
 
         def chosen(found, slot, m):
             rank = jnp.where((slot // CAP) % 2 == m, slot % CAP, 2 * tokens)
@@ -294,17 +300,19 @@
             )
             slot, token = iotas((all_slots, tokens))
             place[m] = jnp.where(chosen(found, slot, m), 1.0, 0.0).astype(jnp.bfloat16)
-            ranks_t, share_t = ranks.T, share.T
-            found = jnp.dot(
-                ranks_t.astype(jnp.bfloat16), spread, preferred_element_type=jnp.float32
-            )
-            token, slot = iotas((tokens, all_slots))
-            here = chosen(found, slot, m)
+            ranks_t, share_t = ranks.T.astype(jnp.bfloat16), share.T
             high = share_t.astype(jnp.bfloat16)
             low = (share_t - high.astype(jnp.float32)).astype(jnp.bfloat16)
-            for i, values in enumerate((high, low)):
-                values = jnp.dot(values, spread, preferred_element_type=jnp.float32)
-                mixers[m, i] = jnp.where(here, values, 0.0).astype(jnp.bfloat16)
+            for g in range(4):
+                chip, slot = iotas((chips, all_slots // 4))
+                spread = jnp.where(slot // slots + g * (chips // 4) == chip, 1.0, 0.0)
+                spread = spread.astype(jnp.bfloat16)
+                found = jnp.dot(ranks_t, spread, preferred_element_type=jnp.float32)
+                token, slot = iotas((tokens, all_slots // 4))
+                here = chosen(found, slot, m)
+                for i, values in enumerate((high, low)):
+                    values = jnp.dot(values, spread, preferred_element_type=jnp.float32)
+                    mixers[g, m, i] = jnp.where(here, values, 0.0).astype(jnp.bfloat16)
 
     def norm_block(j, carry):
         squares = jnp.zeros((tokens, 1), jnp.float32)
@@ -432,32 +440,18 @@
     own = (x_ref[...].astype(jnp.float32) + total).astype(jnp.bfloat16)
 
     mids[c] = own
-    wide = own.astype(jnp.float32)
-    sums[t, c] = jnp.broadcast_to(jnp.sum(wide * wide, axis=1, keepdims=True), (tokens, 128))
-    for i, (dc, dt) in enumerate(others):
-        send(sums.at[t, c], sums.at[t, c], sum_s.at[i], sum_r.at[i], device(dc, 0, 0, dt))
     send(mids.at[c], mids.at[c], mid_s, mid_r, device(1, 0, 0, 0))
     wait_bytes(mids.at[0], mid_r)
-    for i in range(len(others)):
-        wait_bytes(sums.at[0, 0], sum_r.at[i])
-    normed = []
-    gain = gain_expert_ref[pl.ds(pl.multiple_of(t * quarter, 128), quarter)].reshape(1, quarter)
-    for m in range(2):
-        squares = sums[0, m]
-        for q in range(1, tensors):
-            squares += sums[q, m]
-        inverse = lax.rsqrt(squares[:, :1] / full + EPSILON)
-        normed.append((mids[m].astype(jnp.float32) * inverse * gain).astype(jnp.bfloat16))
-
-    per = chips // CHUNKS
-    for chunk in range(CHUNKS):
+
+    for chunk in range(chunks):
         these = pl.ds(chunk * per * slots, per * slots)
-        block = jnp.dot(place[0, these], normed[0], preferred_element_type=jnp.float32)
-        block += jnp.dot(place[1, these], normed[1], preferred_element_type=jnp.float32)
+        block = jnp.dot(place[0, these], mids[0], preferred_element_type=jnp.float32)
+        block += jnp.dot(place[1, these], mids[1], preferred_element_type=jnp.float32)
         block = block.reshape(per, slots, quarter).astype(jnp.bfloat16)
         outgoing[pl.ds(chunk * per, per)] = block
-        if chunk == 0:
-            arrived[t, 0] = block[0]
+        low = chunk * per
+        if low == self_k:
+            arrived[t, self_k] = block[0]
 
         def go(k, carry):
             send(
@@ -465,15 +459,28 @@
                 arrived.at[t, k],
                 go_s.at[k],
                 go_r.at[k],
-                device(0, k // nz, k % nz, 0),
+                device(0, *offset(k), 0),
                 keep=False,
             )
             return carry
 
-        lax.fori_loop(max(chunk * per, 1), (chunk + 1) * per, go, 0)
+        lax.fori_loop(low + (low == self_k), low + per, go, 0)
 
     for load in expert_loads:
         load.wait()
+    for copy in started:
+        copy.wait_send()
+    for i in range(tensors - 1):
+        wait_bytes(along_x.at[i], a1_s.at[i])
+    for dy in range(ny - 1):
+        for q in range(tensors):
+            wait_bytes(along_y.at[dy, q], b1_s.at[dy, q])
+
+    @pl.when(sends_weights)
+    def _():
+        for m in range(3):
+            for copy in first_hop(m):
+                copy.wait_send()
 
     cut = per // 2
     ways = ((right, 1), (left, tensors - 1))
@@ -485,11 +492,15 @@
     def half_of(chunk, way):
         return pl.ds(chunk * per + way * cut, cut)
 
+    def back_to(k):
+        dy, dz = offset(k)
+        return device(0, ny - dy, nz - dz, 0)
+
     def share_chunk(chunk):
         def arrive(i, carry):
             k = chunk * per + i
 
-            @pl.when(k > 0)
+            @pl.when(k != self_k)
             def _():
                 wait_bytes(arrived.at[t, k], go_r.at[k])
 
@@ -514,9 +525,16 @@
             wait_bytes(arrived.at[source, half_of(chunk, way)], f_r.at[way, chunk])
         gate_sums = jnp.zeros((per * slots, hidden_width), jnp.float32)
         upward = jnp.zeros((per * slots, hidden_width), jnp.float32)
+        squares = jnp.zeros((per, slots, 1), jnp.float32)
         for q in range(tensors):
-            values = arrived[q, here].reshape(per * slots, quarter)
+            values = arrived[q, here].astype(jnp.float32)
+            squares += jnp.sum(values * values, axis=2, keepdims=True)
+        inverse = lax.rsqrt(squares / full + EPSILON)
+        for q in range(tensors):
             these = slice(q * quarter, (q + 1) * quarter)
+            gain = gain_expert_ref[these].reshape(1, 1, quarter)
+            values = arrived[q, here].astype(jnp.float32) * inverse * gain
+            values = values.reshape(per * slots, quarter).astype(jnp.bfloat16)
             gate_sums += jnp.dot(values, gate[these], preferred_element_type=jnp.float32)
             upward += jnp.dot(values, up[these], preferred_element_type=jnp.float32)
         hidden = (silu(gate_sums) * upward).astype(jnp.bfloat16)
@@ -563,14 +581,14 @@
         def give(i, carry):
             k = chunk * per + i
 
-            @pl.when(k > 0)
+            @pl.when(k != self_k)
             def _():
                 send(
                     summed.at[k],
                     returned.at[k],
                     back_s.at[k],
                     back_r.at[k],
-                    device(0, ny - k // nz, nz - k % nz, 0),
+                    back_to(k),
                     False,
                 )
 
@@ -583,57 +601,21 @@
     def stage(i, carry):
         for lag, act in work:
 
-            @pl.when((i >= lag) & (i < CHUNKS + lag))
+            @pl.when((i >= lag) & (i < chunks + lag))
             def _(lag=lag, act=act):
                 act(i - lag)
 
         return carry
 
-    lax.fori_loop(0, CHUNKS + len(work) - 1, stage, 0)
-    returned[0] = summed[0]
-
-    def arrive_back(k, carry):
-        wait_bytes(returned.at[k], back_r.at[k])
+    lax.fori_loop(0, chunks + len(work) - 1, stage, 0)
+    returned[self_k] = summed[self_k]
+
+    def sent_rows(k, carry):
+        wait_bytes(outgoing.at[k], go_s.at[k])
         return carry
 
-    mixed = [jnp.zeros((tokens, quarter), jnp.float32) for _ in range(2)]
-    for i in range(2):
-        low, high = i * chips // 2, (i + 1) * chips // 2
-        lax.fori_loop(max(low, 1), high, arrive_back, 0)
-        back = returned[low:high].reshape(all_slots // 2, quarter)
-        for m in range(2):
-            for j in range(2):
-                mixer = mixers[m, j, :, low * slots : high * slots]
-                mixed[m] += jnp.dot(mixer, back, preferred_element_type=jnp.float32)
-    for m in range(2):
-        mixes[0, m] = mixed[m]
-    send(mixes.at[0], mixes.at[1], mix_s, mix_r, device(1, 0, 0, 0))
-    wait_bytes(mixes.at[1], mix_r)
-    for m in range(2):
-        middle = mids[m]
-        final = middle.astype(jnp.float32) + (mixes[0, m] + mixes[1, m])
-        out_ref[m] = jnp.where(c == 0, middle, final.astype(jnp.bfloat16))
-
-    for copy in started:
-        copy.wait_send()
-    for i in range(tensors - 1):
-        wait_bytes(along_x.at[i], a1_s.at[i])
-    for dy in range(ny - 1):
-        for q in range(tensors):
-            wait_bytes(along_y.at[dy, q], b1_s.at[dy, q])
-
-    @pl.when(sends_weights)
-    def _():
-        for m in range(3):
-            for copy in first_hop(m):
-                copy.wait_send()
-
-    def sent(k, carry):
-        wait_bytes(outgoing.at[k], go_s.at[k])
-        wait_bytes(summed.at[k], back_s.at[k])
-        return carry
-
-    lax.fori_loop(1, chips, sent, 0)
+    lax.fori_loop(0, self_k, sent_rows, 0)
+    lax.fori_loop(self_k + 1, chips, sent_rows, 0)
 
     def sent_chunk(chunk, carry):
         for way, dt in ways:
@@ -643,7 +625,38 @@
             wait_bytes(pieces.at[0, some(chunk)], side_s.at[way, chunk])
         return carry
 
-    lax.fori_loop(0, CHUNKS, sent_chunk, 0)
+    lax.fori_loop(0, chunks, sent_chunk, 0)
+
+    def arrive_back(k, carry):
+        wait_bytes(returned.at[k], back_r.at[k])
+        return carry
+
+    mixed = [jnp.zeros((tokens, quarter), jnp.float32) for _ in range(2)]
+    for g in range(4):
+        low, high = g * chips // 4, (g + 1) * chips // 4
+        lax.fori_loop(low, min(high, self_k), arrive_back, 0)
+        lax.fori_loop(max(low, self_k + 1), high, arrive_back, 0)
+        back = returned[low:high].reshape(all_slots // 4, quarter)
+        for m in range(2):
+            for j in range(2):
+                mixed[m] += jnp.dot(mixers[g, m, j], back, preferred_element_type=jnp.float32)
+    for m in range(2):
+        mixes[0, m] = mixed[m]
+    send(mixes.at[0], mixes.at[1], mix_s, mix_r, device(1, 0, 0, 0), False)
+    wait_bytes(mixes.at[1], mix_r)
+    for m in range(2):
+        middle = mids[m]
+        final = middle.astype(jnp.float32) + (mixes[0, m] + mixes[1, m])
+        out_ref[m] = jnp.where(c == 0, middle, final.astype(jnp.bfloat16))
+
+    wait_bytes(mixes.at[0], mix_s)
+
+    def sent(k, carry):
+        wait_bytes(summed.at[k], back_s.at[k])
+        return carry
+
+    lax.fori_loop(0, self_k, sent, 0)
+    lax.fori_loop(self_k + 1, chips, sent, 0)
 
 
 def body(
@@ -699,9 +712,8 @@
             pltpu.VMEM((full, hidden), bf16),
             pltpu.VMEM((hidden, full), bf16),
             pltpu.VMEM((2, chips * slots, tokens), bf16),
-            pltpu.VMEM((2, 2, tokens, chips * slots), bf16),
+            pltpu.VMEM((4, 2, 2, tokens, chips // 4 * slots), bf16),
             pltpu.VMEM((2, tokens, quarter), bf16),
-            pltpu.VMEM((tensors, 2, tokens, 128), f32),
             pltpu.VMEM(sent_rows, bf16),
             pltpu.VMEM((tensors, *sent_rows), bf16),
             pltpu.VMEM((tensors, *sent_rows), bf16),
@@ -729,18 +741,16 @@
             dma((tensors - 1,)),
             dma(()),
             dma(()),
-            dma((2 * tensors - 1,)),
-            dma((2 * tensors - 1,)),
             dma((chips,)),
             dma((chips,)),
-            dma((2, CHUNKS)),
-            dma((2, CHUNKS)),
-            dma((2, CHUNKS)),
-            dma((2, CHUNKS)),
-            dma((2, CHUNKS)),
-            dma((2, CHUNKS)),
-            dma((2, CHUNKS)),
-            dma((2, CHUNKS)),
+            dma((2, 2 * ny)),
+            dma((2, 2 * ny)),
+            dma((2, 2 * ny)),
+            dma((2, 2 * ny)),
+            dma((2, 2 * ny)),
+            dma((2, 2 * ny)),
+            dma((2, 2 * ny)),
+            dma((2, 2 * ny)),
             dma((chips,)),
             dma((chips,)),
             dma(()),

time: 165 us -> 160 us (0.970)
  Pallas kernels: 163 us -> 158 us
    pallas_call x1, Pallas kernels: 163 us -> 158 us  [body(): pl.pallas_call(functools.partial(kernel, split, tensors), out_shape=jax.S...]
where the time goes in v4:
time: 160 us
  Pallas kernels  158 us (99%)
  local copies, waits for them, and re-layouts  1.6 us (1%)
    pallas_call x1, Pallas kernels, body(): pl.pallas_call(functools.partial(kernel, split, tensors), out_shape=jax.S...  158 us

profile of v4, /device:TPU:1, one launch (start us, length us, event | category | flops | bytes accessed | tf_op | source)
XLA Modules:
  0.0 159.8 jit_solution(2443210021847453949)
XLA Ops:
  0.0 158.1 %sections.1 = bf16[2,64,640]{2,1,0:T(8,128)(2,1)} custom-call(bf16[64,640]{1,0:T(8,128)(2,1)} %bitcast.5, s32[6,2,64]{2,1,0:T(2,128)} %bitcast.6, f32[6,2,64]{2,1,0:T(2,128)} %bitcast.7, f32[2560]{0:T(1024)} %gain_dense_ref.1, f32[2560]{0:T(1024)} %gain_expert_ref.1, bf16[80,1536]{1,0:T(8,128)(2,1)} %dense_gate_hbm.1, bf16[80,1536]{1,0:T(8,128)(2,1)} %dense_up_hbm.1, ...), custom_call_target="tpu_custom_call" | custom-call | tf_op jit(solution)/shard_map/sections/pallas_call | solution.py:693
  158.2 1.6 copy.13

commit v5 on v4

--- a/solution.py
+++ b/solution.py
@@ -146,9 +146,8 @@
         load.start()
 
     group = [(dy, dt) for dt in range(tensors) for dy in range(ny) if dy or dt]
-    others = [(dc, dt) for dc in range(2) for dt in range(tensors) if dc or dt]
     offsets = {(0, dy, 0, dt) for dy, dt in group}
-    offsets |= {(dc, 0, 0, dt) for dc, dt in others}
+    offsets |= {(1, 0, 0, 0)}
     offsets |= {(0, dy, dz, 0) for dy in range(ny) for dz in range(nz) if dy or dz}
     greet(sorted(offsets), device)
     for load in dense_loads:
@@ -198,7 +197,6 @@
                 dense_held.at[m, :, columns], wbuf.at[p, m], w1_r.at[lax.rem(y, half), m]
             ).start()
 
-    kinds = (pl.ds(0, 2), pl.ds(2, 1))
     hops = {}
     for a in range(half):
         far, near = nz // 2, (nz - 1) // 2
@@ -209,7 +207,7 @@
 
     def forward(kind, a, direction, step):
         sign = signs[direction]
-        held = wbuf.at[piece(c, a, -sign * (step - 1)), kinds[kind]]
+        held = wbuf.at[piece(c, a, -sign * (step - 1)), kind]
         send(
             held,
             held,
@@ -219,12 +217,11 @@
         )
 
     def hand_over(kind, a, dz):
-        held = wbuf.at[piece(c, a, dz), kinds[kind]]
+        held = wbuf.at[piece(c, a, dz), kind]
         send(held, held, sib_s.at[kind, a, dz % nz], sib_r.at[kind, a, dz % nz], device(1, 0, 0, 0))
 
     def begin(kind, a):
-        for m in range(2) if kind == 0 else (2,):
-            wait_bytes(wbuf.at[piece(c, a, 0), m], w1_r.at[a, m])
+        wait_bytes(wbuf.at[piece(c, a, 0), kind], w1_r.at[a, kind])
         for direction in (right, left):
             if hops[direction, a] >= 1:
                 forward(kind, a, direction, 1)
@@ -236,7 +233,7 @@
                 continue
             sign = signs[direction]
             wait_bytes(
-                wbuf.at[piece(c, a, -sign * step), kinds[kind]],
+                wbuf.at[piece(c, a, -sign * step), kind],
                 ring_r.at[kind, direction, a, step - 1],
             )
             if step + 1 <= hops[direction, a]:
@@ -245,10 +242,11 @@
 
     def from_other_core(kind, a):
         for dz in range(nz):
-            wait_bytes(wbuf.at[piece(1 - c, a, dz), kinds[kind]], sib_r.at[kind, a, dz])
-
-    for a in range(half):
-        begin(0, a)
+            wait_bytes(wbuf.at[piece(1 - c, a, dz), kind], sib_r.at[kind, a, dz])
+
+    for kind in range(2):
+        for a in range(half):
+            begin(kind, a)
 
     for i, (dy, dt) in enumerate(group):
         send(x_ref, xbuf.at[t, y], tok_s.at[i], tok_r.at[i], device(0, dy, 0, dt))
@@ -273,7 +271,22 @@
     def iotas(shape):
         return (lax.broadcasted_iota(jnp.int32, shape, i) for i in range(2))
 
-    def plan_routes():
+    def mix_plan(m, ranks, share, chosen):
+        ranks_t, share_t = ranks.T.astype(jnp.bfloat16), share.T
+        high = share_t.astype(jnp.bfloat16)
+        low = (share_t - high.astype(jnp.float32)).astype(jnp.bfloat16)
+        for g in range(4):
+            chip, slot = iotas((chips, all_slots // 4))
+            spread = jnp.where(slot // slots + g * (chips // 4) == chip, 1.0, 0.0)
+            spread = spread.astype(jnp.bfloat16)
+            found = jnp.dot(ranks_t, spread, preferred_element_type=jnp.float32)
+            token, slot = iotas((tokens, all_slots // 4))
+            here = chosen(found, slot, m)
+            for i, values in enumerate((high, low)):
+                values = jnp.dot(values, spread, preferred_element_type=jnp.float32)
+                mixers[g, m, i] = jnp.where(here, values, 0.0).astype(jnp.bfloat16)
+
+    def plan_routes(mixing):
         experts = expert_at(lax.broadcasted_iota(jnp.int32, (chips, tokens), 0))
         one, two = iotas((tokens, tokens))
         before = jnp.where(one < two, 1.0, 0.0).astype(jnp.bfloat16)
@@ -295,24 +308,14 @@
                 named.astype(jnp.bfloat16), before, preferred_element_type=jnp.float32
             )
             ranks = jnp.where(named > 0.5, ranks, -1.0)
+            if mixing:
+                mix_plan(m, ranks, share, chosen)
+                continue
             found = jnp.dot(
                 spread_t, ranks.astype(jnp.bfloat16), preferred_element_type=jnp.float32
             )
             slot, token = iotas((all_slots, tokens))
             place[m] = jnp.where(chosen(found, slot, m), 1.0, 0.0).astype(jnp.bfloat16)
-            ranks_t, share_t = ranks.T.astype(jnp.bfloat16), share.T
-            high = share_t.astype(jnp.bfloat16)
-            low = (share_t - high.astype(jnp.float32)).astype(jnp.bfloat16)
-            for g in range(4):
-                chip, slot = iotas((chips, all_slots // 4))
-                spread = jnp.where(slot // slots + g * (chips // 4) == chip, 1.0, 0.0)
-                spread = spread.astype(jnp.bfloat16)
-                found = jnp.dot(ranks_t, spread, preferred_element_type=jnp.float32)
-                token, slot = iotas((tokens, all_slots // 4))
-                here = chosen(found, slot, m)
-                for i, values in enumerate((high, low)):
-                    values = jnp.dot(values, spread, preferred_element_type=jnp.float32)
-                    mixers[g, m, i] = jnp.where(here, values, 0.0).astype(jnp.bfloat16)
 
     def norm_block(j, carry):
         squares = jnp.zeros((tokens, 1), jnp.float32)
@@ -371,23 +374,26 @@
     steps = nz // 2
     early = max(steps - 1, 1)
     for step in range(1, steps + 1):
-        for a in range(half):
-            ring(0, a, step)
+        for kind in range(2):
+            for a in range(half):
+                ring(kind, a, step)
+        if step == max(steps - 2, 1):
+            begin(2, 0)
+        if step == early and half > 1:
+            begin(2, half - 1)
         if step == early:
-            begin(1, 0)
             for i in range(len(group)):
                 wait_bytes(xbuf.at[0, 0], tok_r.at[i])
             lax.fori_loop(0, ny, norm_block, 0)
-        if step == steps and half > 1:
-            begin(1, half - 1)
     left_over = list(range(tensors))
     for step in range(1, steps + 1):
-        ring(1, 0, step)
+        ring(2, 0, step)
         if half > 1 and step < steps:
-            ring(1, half - 1, step)
+            ring(2, half - 1, step)
         if step == 1:
             for a in range(half):
                 from_other_core(0, a)
+                from_other_core(1, a)
         if step < steps and left_over:
             add_quarter(left_over.pop(0))
     for q in left_over:
@@ -395,11 +401,11 @@
     hidden_ref[...] = (silu(acc[0]) * acc[1]).astype(jnp.bfloat16)
     for a in range(half):
         if a:
-            ring(1, a, steps)
-        from_other_core(1, a)
+            ring(2, a, steps)
+        from_other_core(2, a)
         for q in quarters(a):
             give_quarter(q)
-    plan_routes()
+    plan_routes(False)
 
     total = part[t, :, first].astype(jnp.float32)
     for i in range(tensors - 1):
@@ -468,19 +474,6 @@
 
     for load in expert_loads:
         load.wait()
-    for copy in started:
-        copy.wait_send()
-    for i in range(tensors - 1):
-        wait_bytes(along_x.at[i], a1_s.at[i])
-    for dy in range(ny - 1):
-        for q in range(tensors):
-            wait_bytes(along_y.at[dy, q], b1_s.at[dy, q])
-
-    @pl.when(sends_weights)
-    def _():
-        for m in range(3):
-            for copy in first_hop(m):
-                copy.wait_send()
 
     cut = per // 2
     ways = ((right, 1), (left, tensors - 1))
@@ -598,12 +591,35 @@
 
     work = ((0, share_chunk), (1, forward_chunk), (2, compute_chunk), (3, relay_chunk), (4, return_chunk))
 
+    def dense_sent():
+        for copy in started:
+            copy.wait_send()
+        for i in range(tensors - 1):
+            wait_bytes(along_x.at[i], a1_s.at[i])
+        for dy in range(ny - 1):
+            for q in range(tensors):
+                wait_bytes(along_y.at[dy, q], b1_s.at[dy, q])
+
+        @pl.when(sends_weights)
+        def _():
+            for m in range(3):
+                for copy in first_hop(m):
+                    copy.wait_send()
+
     def stage(i, carry):
         for lag, act in work:
 
             @pl.when((i >= lag) & (i < chunks + lag))
             def _(lag=lag, act=act):
                 act(i - lag)
+
+        @pl.when(i == chunks // 2)
+        def _():
+            plan_routes(True)
+
+        @pl.when(i == chunks // 2 + 1)
+        def _():
+            dense_sent()
 
         return carry
 
@@ -727,10 +743,10 @@
             dma((group,)),
             dma((ny - 1, 3)),
             dma((half, 3)),
-            dma((2, 2, half, steps)),
-            dma((2, 2, half, steps)),
-            dma((2, half, nz)),
-            dma((2, half, nz)),
+            dma((3, 2, half, steps)),
+            dma((3, 2, half, steps)),
+            dma((3, half, nz)),
+            dma((3, half, nz)),
             dma((tensors - 1,)),
             dma((tensors - 1,)),
             dma((ny - 1, tensors)),

time: 160 us -> 156 us (0.975)
  Pallas kernels: 158 us -> 154 us
    pallas_call x1, Pallas kernels: 158 us -> 154 us  [body(): pl.pallas_call(functools.partial(kernel, split, tensors), out_shape=jax.S...]
where the time goes in v5:
time: 156 us
  Pallas kernels  154 us (99%)
  local copies, waits for them, and re-layouts  1.6 us (1%)
    pallas_call x1, Pallas kernels, body(): pl.pallas_call(functools.partial(kernel, split, tensors), out_shape=jax.S...  154 us

profile of v5, /device:TPU:1, one launch (start us, length us, event | category | flops | bytes accessed | tf_op | source)
XLA Modules:
  0.0 155.6 jit_solution(14845261836038565780)
XLA Ops:
  0.0 154.0 %sections.1 = bf16[2,64,640]{2,1,0:T(8,128)(2,1)} custom-call(bf16[64,640]{1,0:T(8,128)(2,1)} %bitcast.5, s32[6,2,64]{2,1,0:T(2,128)} %bitcast.6, f32[6,2,64]{2,1,0:T(2,128)} %bitcast.7, f32[2560]{0:T(1024)} %gain_dense_ref.1, f32[2560]{0:T(1024)} %gain_expert_ref.1, bf16[80,1536]{1,0:T(8,128)(2,1)} %dense_gate_hbm.1, bf16[80,1536]{1,0:T(8,128)(2,1)} %dense_up_hbm.1, ...), custom_call_target="tpu_custom_call" | custom-call | tf_op jit(solution)/shard_map/sections/pallas_call | solution.py:709
  154.0 1.6 %copy.13 = bf16[1,2,64,640]{3,2,1,0:T(8,128)(2,1)} copy(bf16[1,2,64,640]{3,2,1,0:T(8,128)(2,1)} %bitcast.4) | data formatting | bytes 327680

commit v6 on v5

--- a/solution.py
+++ b/solution.py
@@ -589,7 +589,7 @@
 
         lax.fori_loop(0, per, give, 0)
 
-    work = ((0, share_chunk), (1, forward_chunk), (2, compute_chunk), (3, relay_chunk), (4, return_chunk))
+    work = ((0, share_chunk), (2, forward_chunk), (3, compute_chunk), (4, relay_chunk), (5, return_chunk))
 
     def dense_sent():
         for copy in started:
@@ -623,7 +623,7 @@
 
         return carry
 
-    lax.fori_loop(0, chunks + len(work) - 1, stage, 0)
+    lax.fori_loop(0, chunks + len(work), stage, 0)
     returned[self_k] = summed[self_k]
 
     def sent_rows(k, carry):

time: 156 us -> 156 us (level)
  no operation moved by 1% of the time
where the time goes in v6:
time: 156 us
  Pallas kernels  154 us (99%)
  local copies, waits for them, and re-layouts  1.6 us (1%)
    pallas_call x1, Pallas kernels, body(): pl.pallas_call(functools.partial(kernel, split, tensors), out_shape=jax.S...  154 us

profile of v6, /device:TPU:1, one launch (start us, length us, event | category | flops | bytes accessed | tf_op | source)
XLA Modules:
  0.0 155.8 jit_solution(12087884181218932343)
XLA Ops:
  0.0 154.2 %sections.1 = bf16[2,64,640]{2,1,0:T(8,128)(2,1)} custom-call(bf16[64,640]{1,0:T(8,128)(2,1)} %bitcast.5, s32[6,2,64]{2,1,0:T(2,128)} %bitcast.6, f32[6,2,64]{2,1,0:T(2,128)} %bitcast.7, f32[2560]{0:T(1024)} %gain_dense_ref.1, f32[2560]{0:T(1024)} %gain_expert_ref.1, bf16[80,1536]{1,0:T(8,128)(2,1)} %dense_gate_hbm.1, bf16[80,1536]{1,0:T(8,128)(2,1)} %dense_up_hbm.1, ...), custom_call_target="tpu_custom_call" | custom-call | tf_op jit(solution)/shard_map/sections/pallas_call | solution.py:709
  154.2 1.6 %copy.13 = bf16[1,2,64,640]{3,2,1,0:T(8,128)(2,1)} copy(bf16[1,2,64,640]{3,2,1,0:T(8,128)(2,1)} %bitcast.4) | data formatting | bytes 327680
